TPU v7x, 128 devices: a whole 4x4x4 slice. The times are simulated.
128 devices in a mesh: grp: 4 (over y), dev: 32 (over z, x, core).
Axes of the slice: x: 4, y: 4, z: 4, core: 2. Of those that a mesh axis runs over, the one named last changes fastest.
Arguments:
- strain: bfloat16 [16384, 30720], P('grp', 'dev'), may hold values from -6 to 6
- taps: bfloat16 [64], replicated, may hold values from -0.75 to 0.75
- tiles: int32 [4160, 2], replicated, may hold values from 0 to 2047, as said below
- owner: int32 [4160], replicated, may hold values from 0 to 127, as said below
Outputs:
- correlation: float32 [8192, 8, 8, 384], P(('grp', 'dev'))
Inputs may be any that keep to these rules, and one draw needn't show every extreme that they name: The two blocks of a tile lie in different groups of 128 consecutive channels, and for every owner all block entries of its tiles lie in pairwise different such groups; the busiest owners use every group. `owner`: two owners hold 1 tile, two hold 2, and so on up to two that hold 64; which owners these are is drawn at random, and the list is in random order.
All inputs are finite; a program needn't handle non-finite values.
Results may differ from a plain program's by a relative error of at most 0.0083.
Values may be sent and summed in bfloat16 or wider, within the bound.
A program may use at most 128 MiB of HBM per device.

v0:
```python
import functools
import math

import jax
import jax.numpy as jnp
import ml_dtypes
import numpy as np
from jax import lax
from jax.experimental import pallas as pl
from jax.experimental.pallas import tpu as pltpu
from jax.sharding import PartitionSpec as P

NT = 6144
NF = 1024
F0 = 32
NLAG = 384
NTAP = 64
DECIM = 5
BLK = 8
MEMBERS = 32
GROUPS = 4
DEVICES = 128
COLS = NT // MEMBERS
EXT = 208
PARTS = 8
CH = 128
SLOTS = 64
PIECE = 128
PIECES = NF // PIECE
CUTS = (0, 4, 6, 8)
COUNTS = (4, 2, 2)
TILES = 4
MESH = pl.DeviceIdType.MESH
F32 = jnp.float32
BF16 = jnp.bfloat16


def trig(phase, factor=1.0):
    angle = np.float32(2.0 * math.pi / NT) * phase.astype(np.float32)
    angle = angle.astype(np.float64)
    return np.cos(angle) * factor, -np.sin(angle) * factor


def base_table():
    rows = (np.arange(4)[:, None] * COLS + np.arange(EXT)[None, :]).reshape(-1)
    phase = rows[:, None] * (F0 + np.arange(NF))[None, :] % NT
    real, imag = trig(phase)
    return np.concatenate([real, imag], axis=1).astype(ml_dtypes.bfloat16)


def turns(part):
    eighth = part * lax.broadcasted_iota(jnp.int32, (1, NF), 1) % 8
    half = math.sqrt(0.5)

    def wave(eighth):
        size = jnp.where(eighth % 4 == 0, 1.0, jnp.where(eighth % 4 == 2, 0.0, half))
        return jnp.where((eighth >= 3) & (eighth <= 5), -size, size)

    return wave(eighth), wave((eighth + 6) % 8)


def lag_table():
    lags = (np.arange(NLAG) - NLAG // 2) % NT
    phase = (F0 + np.arange(NF))[:, None] * lags[None, :] % NT
    real, imag = trig(phase, 1.0 / math.sqrt(NF))
    return np.concatenate([real, imag], axis=0).astype(ml_dtypes.bfloat16)


def nt_dot(a, b):
    return lax.dot_general(a, b, (((1,), (1,)), ((), ())), preferred_element_type=F32)


def stack_rows(pieces, rows, fill):
    width = sum(piece.shape[1] for piece in pieces)
    extra = jnp.full((1, rows * 128 - width), fill, jnp.int32)
    line = jnp.concatenate([*pieces, extra], axis=1)
    return jnp.concatenate(
        [line[:, index * 128 : (index + 1) * 128] for index in range(rows)], axis=0
    )


def make_band(member, taps):
    tap = lax.broadcasted_iota(jnp.int32, (NTAP, 1024), 0)
    lane = lax.broadcasted_iota(jnp.int32, (NTAP, 1024), 1)
    place = (lane == (1024 - tap) % 1024).astype(F32).astype(BF16)
    taps = jnp.broadcast_to(taps.astype(F32), (8, NTAP)).astype(BF16)
    line = jnp.dot(taps, place, preferred_element_type=F32)
    first_rows = pltpu.roll(line, 0, 1, stride=DECIM, stride_axis=0)
    band = jnp.concatenate(
        [pltpu.roll(first_rows, 8 * DECIM * index, 1) for index in range(EXT // 8)], axis=0
    )
    row = lax.broadcasted_iota(jnp.int32, (EXT, 1024), 0)
    limit = jnp.where(member == MEMBERS - 1, COLS, 205)
    return jnp.where(row < limit, band, 0.0)[:, :960].astype(BF16)


def coordinates(device):
    return device // 8 % 4, device // 2 % 4, device // 32, device % 2


def line_and_place(device, axis):
    z, x, y, c = coordinates(device)
    if axis == 0:
        return y * 8 + x * 2 + c, z
    if axis == 1:
        return y * 8 + z * 2 + c, x
    return z * 8 + x * 2 + c, y


def device_of(line, place, axis):
    first, second, c = line // 8, line // 2 % 4, line % 2
    if axis == 0:
        return first * 32 + place * 8 + second * 2 + c
    if axis == 1:
        return first * 32 + second * 8 + place * 2 + c
    return place * 32 + line


def make_plan(me, src, dst, own, plan_ref):
    rows = src.shape[0]
    mine = own == me
    lane_a = lax.broadcasted_iota(jnp.int32, (128, 128), 0)
    lane = lax.broadcasted_iota(jnp.int32, (rows, 128), 1)
    row = lax.broadcasted_iota(jnp.int32, (rows, 128), 0)
    flags = jnp.where(mine, 1, 0)
    within = flags
    for shift in (1, 2, 4, 8, 16, 32, 64):
        within = within + jnp.where(lane >= shift, pltpu.roll(within, shift, 1), 0)
    totals = jnp.broadcast_to(jnp.sum(flags, axis=1, keepdims=True), (rows, 128))
    before = totals
    for shift in (1, 2, 4, 8, 16, 32):
        before = before + jnp.where(row >= shift, pltpu.roll(before, shift, 0), 0)
    slot = jnp.where(mine, within - flags + before - totals, -1)
    src_dev, dst_dev = src // 16, dst // 16

    first = jnp.zeros((SLOTS, 128), jnp.int32)
    second = jnp.zeros((SLOTS, 128), jnp.int32)
    for index in range(rows):
        hit = slot[index : index + 1, :] == lane_a[:SLOTS]
        first = first + jnp.where(hit, src_dev[index : index + 1, :], 0)
        second = second + jnp.where(hit, dst_dev[index : index + 1, :], 0)
    ends = jnp.sum(jnp.concatenate([first, second], axis=0).T, axis=0, keepdims=True)
    lines = []
    for axis in range(3):
        line, place = line_and_place(ends, axis)
        lines.append(line * 4 + place)
    count = jnp.sum(flags, axis=(0, 1), keepdims=True)
    lines.append(jnp.broadcast_to(count, (1, 128)))
    plan_ref[12:16, :] = jnp.concatenate(lines, axis=0)

    z, x, y, _ = coordinates(me)

    def wanted(entry, _):
        axis, place = entry // 4, entry % 4
        source = jnp.where(
            axis == 0, me + (place - z) * 8, jnp.where(axis == 1, me + (place - x) * 2, me + (place - y) * 32)
        )
        local = jnp.where(src_dev == source, src % 16, 0) + jnp.where(dst_dev == source, dst % 16, 0)
        blocks = jnp.zeros((128, 128), jnp.int32)
        for index in range(rows):
            hit = own[index : index + 1, :] == lane_a
            blocks = blocks + jnp.where(hit, local[index : index + 1, :], 0)
        plan_ref[pl.ds(entry, 1), :] = jnp.sum(blocks.T, axis=0, keepdims=True)
        return 0

    lax.fori_loop(0, 12, wanted, 0)


def cross_spectra(into, plan, cross, slot, tile, axes):
    width = len(axes) * PIECE
    for index, axis in enumerate(axes):
        a = into[index, plan[12 + axis, slot]].astype(F32)
        b = into[index, plan[12 + axis, SLOTS + slot]].astype(F32)
        ar, ai, br, bi = a[:BLK], a[BLK:], b[:BLK], b[BLK:]
        left = index * PIECE
        for pair in range(BLK // 2):
            reals, imags = [], []
            for i in (2 * pair, 2 * pair + 1):
                xr, xi = ar[i : i + 1, :], ai[i : i + 1, :]
                reals.append(xr * br + xi * bi)
                imags.append(xi * br - xr * bi)
            at = tile * 64 + pair * 16
            cross[at : at + 16, left : left + PIECE] = jnp.concatenate(reals, axis=0).astype(BF16)
            cross[at : at + 16, width + left : width + left + PIECE] = jnp.concatenate(
                imags, axis=0
            ).astype(BF16)


def axes_of(part):
    return [piece % 3 for piece in range(CUTS[part], CUTS[part + 1])]


def exchange_kernel(
    strain_ref, taps_hbm, tiles_hbm, owner_hbm, base_ref, lag0_ref, lag1_ref,
    late_ref, partial_ref, plan_out_ref,
    raw, taps_ref, tiles_ref, owner_ref, base, lag0, lag1, band, plan_vector, plan, send, recv, acc,
    gathered0, gathered1, gathered2, gathered3, gathered4, gathered5, gathered6, gathered7,
    out0, out1, out2, in0, in1, cross0, cross1, first_sums, partial,
    raw_sem, small_sem, base_sem, lag_sem, plan_sem, plan_out_sem, send_sem, recv_sem,
    line_sem, gather_sem, out_sem, in_sem, own_sem, partial_sem, plane_sem,
):
    grp, dev = lax.axis_index("grp"), lax.axis_index("dev")
    me = grp * MEMBERS + dev
    chip, core = dev // 2, dev % 2
    zc, xc = chip // 4, chip % 4

    def turned(offset):
        return jnp.where(core == 0, offset, (4 - offset) % 4)

    def at(z, x, c):
        return z % 4 * 8 + x % 4 * 2 + c

    def chip_at(offset):
        return (zc + turned(offset // 4)) % 4 * 4 + (xc + turned(offset % 4)) % 4

    def raw_copy(offset):
        to_chip = chip_at(offset)
        return pltpu.make_async_copy(
            strain_ref.at[:, pl.ds(pl.multiple_of(to_chip * 256, 256), 256)],
            raw.at[to_chip], raw_sem.at[to_chip],
        )

    def fetch(step, _):
        raw_copy(step * 7 % 16).start()
        return 0

    small = ((taps_hbm, taps_ref), (tiles_hbm, tiles_ref), (owner_hbm, owner_ref))
    small_copies = [
        pltpu.make_async_copy(source, into, small_sem.at[index])
        for index, (source, into) in enumerate(small)
    ]
    for copy in small_copies:
        copy.start()
    lax.fori_loop(0, 16, fetch, 0)
    base_copy = pltpu.make_async_copy(base_ref, base, base_sem)
    base_copy.start()
    lag_copies = [
        pltpu.make_async_copy(lag0_ref, lag0, lag_sem.at[0]),
        pltpu.make_async_copy(lag1_ref, lag1, lag_sem.at[1]),
    ]
    for copy in lag_copies:
        copy.start()

    barrier = pltpu.get_barrier_semaphore()

    def greet(step, _):
        pl.semaphore_signal(
            barrier, inc=1, device_id=(grp, (dev + step) % MEMBERS), device_id_type=MESH
        )
        return 0

    lax.fori_loop(1, MEMBERS, greet, 0)
    for step in range(1, GROUPS):
        pl.semaphore_signal(
            barrier, inc=1, device_id=((grp + step) % GROUPS, dev), device_id_type=MESH
        )
    small_copies[0].wait()
    band[...] = make_band(dev, taps_ref[...])
    pl.semaphore_wait(barrier, MEMBERS - 1 + GROUPS - 1)

    def samples_to(to):
        return pltpu.make_async_remote_copy(
            src_ref=send.at[to], dst_ref=recv.at[dev], send_sem=send_sem.at[to],
            recv_sem=recv_sem.at[dev], device_id=(grp, to), device_id_type=MESH,
        )

    def decimate(pair, _):
        results = []
        for index in range(2):
            offset = (pair * 2 + index) * 7 % 16
            raw_copy(offset).wait()
            to_chip = chip_at(offset)
            result = jnp.dot(band[...], raw[to_chip], preferred_element_type=F32)
            results.append((to_chip, result.astype(BF16)))
        for to_chip, result in results:
            for half in range(2):
                to = to_chip * 2 + half
                send[to] = result[:, half * CH : (half + 1) * CH]

                @pl.when(to != dev)
                def _():
                    samples_to(to).start()

        return 0

    lax.fori_loop(0, 8, decimate, 0)
    recv[dev] = send[dev]
    for step in range(1, GROUPS):
        pl.semaphore_signal(
            plane_sem, inc=1, device_id=((grp + step) % GROUPS, dev), device_id_type=MESH
        )
    for copy in small_copies[1:]:
        copy.wait()
    tile_rows = [stack_rows([tiles_ref[side : side + 1, :]], 40, 0) for side in range(2)]
    owner_rows = stack_rows([owner_ref[...].reshape(1, -1)], 40, -1)
    make_plan(me, *tile_rows, owner_rows, plan_vector)
    plan_copy = pltpu.make_async_copy(plan_vector, plan, plan_sem)
    plan_copy.start()
    plan_out = pltpu.make_async_copy(plan_vector, plan_out_ref, plan_out_sem)
    plan_out.start()
    base_copy.wait()
    acc[...] = jnp.zeros_like(acc)

    def transform(step, _):
        offset = step * 7 % 16
        from_chip = (zc - offset // 4 + 4) % 4 * 4 + (xc - offset % 4 + 4) % 4
        for half in range(2):
            source = from_chip * 2 + half

            @pl.when(source != dev)
            def _():
                pltpu.make_async_remote_copy(
                    src_ref=send.at[source], dst_ref=recv.at[source],
                    send_sem=send_sem.at[source], recv_sem=recv_sem.at[source],
                    device_id=(grp, source), device_id_type=MESH,
                ).wait_recv()

        samples = recv[pl.ds(from_chip * 2, 2)].reshape(2 * EXT, CH)
        part = from_chip // 2
        cosine, sine = turns(part)
        table = base[pl.ds(pl.multiple_of(from_chip % 2 * (2 * EXT), 2 * EXT), 2 * EXT), :]
        result = lax.dot_general(
            samples, table, (((0,), (0,)), ((), ())), preferred_element_type=F32
        )
        real, imag = result[:, :NF], result[:, NF:]
        acc[:, :NF] += real * cosine + imag * sine
        acc[:, NF:] += imag * cosine - real * sine
        return 0

    lax.fori_loop(0, 16, transform, 0)

    real, imag = acc[:, :NF], acc[:, NF:]
    power = real * real + imag * imag
    level = jnp.mean(power, axis=1, keepdims=True)
    scale = lax.rsqrt(power + level + 1e-06)
    whitened = jnp.concatenate(
        [(real * scale).reshape(16, BLK, NF), (imag * scale).reshape(16, BLK, NF)], axis=1
    ).astype(BF16)
    outs, ins = (out0, out1, out2), (in0, in1, late_ref)
    gathered = (gathered0, gathered1, gathered2, gathered3)
    gathered = gathered + (gathered4, gathered5, gathered6, gathered7)
    pl.semaphore_wait(plane_sem, GROUPS - 1)
    for piece in range(PIECES):
        line, place = line_and_place(me, piece % 3)
        gathered[piece][place] = whitened[:, :, piece * PIECE : (piece + 1) * PIECE]
        for step in (1, 3, 2):
            to = device_of(line, (place + step) % 4, piece % 3)
            pltpu.make_async_remote_copy(
                src_ref=gathered[piece].at[place], dst_ref=gathered[piece].at[place],
                send_sem=line_sem.at[piece], recv_sem=gather_sem.at[piece],
                device_id=(to // MEMBERS, to % MEMBERS), device_id_type=MESH,
            ).start()

    def select(piece, to, out):
        axis = piece % 3
        for place in range(4):
            out[place] = gathered[piece][place, plan[4 * axis + place, to]]

    def emit(piece, part):
        axis, index = piece % 3, piece - CUTS[part]
        line, place = line_and_place(me, axis)
        first, second = line // 8, line // 2 % 4

        def one(step, _):
            offset = step * 11 % 32
            to_line = (first + turned(offset // 8)) % 4 * 8 + (second + turned(offset // 2 % 4)) % 4 * 2
            to = device_of(to_line + (core + offset) % 2, place, axis)
            select(piece, to, outs[part].at[index, step])
            pltpu.make_async_remote_copy(
                src_ref=outs[part].at[index, step], dst_ref=ins[part].at[index, pl.ds(line * 4, 4)],
                send_sem=out_sem.at[part], recv_sem=in_sem.at[part],
                device_id=(to // MEMBERS, to % MEMBERS), device_id_type=MESH,
            ).start()
            return 0

        lax.fori_loop(1, MEMBERS, one, 0)
        select(piece, me, outs[part].at[index, 0])
        return pltpu.make_async_copy(
            outs[part].at[index, 0], ins[part].at[index, pl.ds(line * 4, 4)], own_sem.at[piece]
        )

    plan_copy.wait()
    own_copies = []
    for part in range(3):
        for piece in range(CUTS[part], CUTS[part + 1]):
            others = gathered[piece].at[pl.ds(0, 3)]
            pltpu.make_async_copy(others, others, gather_sem.at[piece]).wait()
            own_copies.append(emit(piece, part))
            own_copies[piece].start()

    def drain(step, _):
        samples_to((dev + step) % MEMBERS).wait_send()
        return 0

    lax.fori_loop(1, MEMBERS, drain, 0)
    def await_part(part):
        for piece in range(CUTS[part], CUTS[part + 1]):
            own_copies[piece].wait()
        others = ins[part].at[:, pl.ds(0, DEVICES - 4)]
        pltpu.make_async_copy(others, others, in_sem.at[part]).wait()

    def lagged_tiles(group, into, cross, lag, part):
        for tile in range(TILES):
            cross_spectra(into, plan, cross, group * TILES + tile, tile, axes_of(part))
        lagged = jnp.dot(cross[...], lag[...], preferred_element_type=F32)
        return lagged.reshape(TILES, BLK, BLK, NLAG)

    def first_tiles(group, _):
        first_sums[pl.ds(group * TILES, TILES)] = lagged_tiles(group, in0, cross0, lag0, 0)
        return 0

    def second_tiles(group, _):
        rows = pl.ds(group * TILES, TILES)
        partial[rows] = (first_sums[rows] + lagged_tiles(group, in1, cross1, lag1, 1)).astype(BF16)
        pltpu.make_async_copy(partial.at[rows], partial_ref.at[rows], partial_sem).start()
        return 0

    for copy in lag_copies:
        copy.wait()
    await_part(0)
    lax.fori_loop(0, SLOTS // TILES, first_tiles, 0)
    await_part(1)
    lax.fori_loop(0, SLOTS // TILES, second_tiles, 0)
    pltpu.make_async_copy(partial, partial_ref, partial_sem).wait()
    plan_out.wait()
    for part in range(3):
        sent = outs[part].at[:, pl.ds(0, MEMBERS - 1)]
        pltpu.make_async_copy(sent, sent, out_sem.at[part]).wait()
    await_part(2)
    for piece in range(PIECES):
        others = gathered[piece].at[pl.ds(0, 3)]
        pltpu.make_async_copy(others, others, line_sem.at[piece]).wait()


def late_kernel(
    plan_ref, late_ref, partial_ref, lag_ref, out_ref,
    late, lag, partial, total, cross, late_sem, lag_sem, in_sem, out_sem,
):
    count = plan_ref[15, 0]
    pieces = 4
    size = DEVICES // 2
    late_copies = [
        pltpu.make_async_copy(
            late_ref.at[index // 2, pl.ds(size * (index % 2), size)],
            late.at[index // 2, pl.ds(size * (index % 2), size)],
            late_sem.at[index],
        )
        for index in range(pieces)
    ]
    lag_copy = pltpu.make_async_copy(lag_ref, lag, lag_sem)

    def rows(group):
        return pl.ds(group * TILES, TILES)

    def load(group):
        return pltpu.make_async_copy(
            partial_ref.at[rows(group)], partial.at[rows(group)], in_sem.at[group]
        )

    for copy in late_copies:
        copy.start()
    lag_copy.start()

    def fetch(group, _):
        load(group).start()
        return 0

    lax.fori_loop(0, SLOTS // TILES, fetch, 0)
    for copy in late_copies:
        copy.wait()
    lag_copy.wait()

    def one(group, _):
        load(group).wait()

        @pl.when(group * TILES < count)
        def _():
            for tile in range(TILES):
                cross_spectra(late, plan_ref, cross, group * TILES + tile, tile, axes_of(2))
            lagged = jnp.dot(cross[...], lag[...], preferred_element_type=F32)
            lagged = lagged + partial[rows(group)].astype(F32).reshape(lagged.shape)
            index = lax.broadcasted_iota(jnp.int32, lagged.shape, 0) // 64 + group * TILES
            total[rows(group)] = jnp.where(index < count, lagged, 0.0).reshape(TILES, BLK, BLK, NLAG)

        @pl.when(group * TILES >= count)
        def _():
            total[rows(group)] = jnp.zeros((TILES, BLK, BLK, NLAG), F32)

        pltpu.make_async_copy(total.at[rows(group)], out_ref.at[rows(group)], out_sem).start()
        return 0

    lax.fori_loop(0, SLOTS // TILES, one, 0)
    pltpu.make_async_copy(total, out_ref, out_sem).wait()


def per_device(strain, taps, tiles, owner):
    hbm = pl.BlockSpec(memory_space=pl.ANY)
    lag = lag_table()
    lags = [
        lag.reshape(2, PIECES, PIECE, NLAG)[:, CUTS[part] : CUTS[part + 1]].reshape(-1, NLAG)
        for part in range(3)
    ]
    groups = SLOTS // TILES
    late, partial, plan = pl.pallas_call(
        exchange_kernel,
        out_shape=(
            jax.ShapeDtypeStruct((COUNTS[2], DEVICES, 2 * BLK, PIECE), BF16),
            jax.ShapeDtypeStruct((SLOTS, BLK, BLK, NLAG), BF16),
            jax.ShapeDtypeStruct((16, 128), jnp.int32),
        ),
        in_specs=[hbm] * 7,
        out_specs=(hbm, hbm, hbm),
        scratch_shapes=[
            pltpu.VMEM((16, 960, 256), BF16),
            pltpu.VMEM((1, NTAP), BF16),
            pltpu.VMEM((2, 4160), jnp.int32),
            pltpu.VMEM((4160,), jnp.int32),
            pltpu.VMEM((4 * EXT, 2 * NF), BF16),
            pltpu.VMEM((2 * COUNTS[0] * PIECE, NLAG), BF16),
            pltpu.VMEM((2 * COUNTS[1] * PIECE, NLAG), BF16),
            pltpu.VMEM((EXT, 960), BF16),
            pltpu.VMEM((16, 128), jnp.int32),
            pltpu.SMEM((16, 128), jnp.int32),
            pltpu.VMEM((MEMBERS, EXT, CH), BF16),
            pltpu.VMEM((MEMBERS, EXT, CH), BF16),
            pltpu.VMEM((CH, 2 * NF), F32),
            *[pltpu.VMEM((4, 16, 2 * BLK, PIECE), BF16) for _ in range(PIECES)],
            *[pltpu.VMEM((count, MEMBERS, 4, 2 * BLK, PIECE), BF16) for count in COUNTS],
            *[pltpu.VMEM((count, DEVICES, 2 * BLK, PIECE), BF16) for count in COUNTS[:2]],
            *[pltpu.VMEM((TILES * 64, 2 * count * PIECE), BF16) for count in COUNTS[:2]],
            pltpu.VMEM((SLOTS, BLK, BLK, NLAG), F32),
            pltpu.VMEM((SLOTS, BLK, BLK, NLAG), BF16),
            pltpu.SemaphoreType.DMA((16,)),
            pltpu.SemaphoreType.DMA((3,)),
            pltpu.SemaphoreType.DMA,
            pltpu.SemaphoreType.DMA((2,)),
            pltpu.SemaphoreType.DMA,
            pltpu.SemaphoreType.DMA,
            pltpu.SemaphoreType.DMA((MEMBERS,)),
            pltpu.SemaphoreType.DMA((MEMBERS,)),
            pltpu.SemaphoreType.DMA((PIECES,)),
            pltpu.SemaphoreType.DMA((PIECES,)),
            pltpu.SemaphoreType.DMA((3,)),
            pltpu.SemaphoreType.DMA((3,)),
            pltpu.SemaphoreType.DMA((PIECES,)),
            pltpu.SemaphoreType.DMA,
            pltpu.SemaphoreType.REGULAR,
        ],
        compiler_params=pltpu.CompilerParams(
            collective_id=0, has_side_effects=True, vmem_limit_bytes=60 * 2**20
        ),
    )(
        strain.T, taps[None, :], tiles.T, owner, jnp.asarray(base_table()),
        jnp.asarray(lags[0]), jnp.asarray(lags[1]),
    )

    return pl.pallas_call(
        late_kernel,
        out_shape=jax.ShapeDtypeStruct((SLOTS, BLK, BLK, NLAG), F32),
        in_specs=[pl.BlockSpec(memory_space=pltpu.SMEM), hbm, hbm, hbm],
        out_specs=hbm,
        scratch_shapes=[
            pltpu.VMEM((COUNTS[2], DEVICES, 2 * BLK, PIECE), BF16),
            pltpu.VMEM((2 * COUNTS[2] * PIECE, NLAG), BF16),
            pltpu.VMEM((SLOTS, BLK, BLK, NLAG), BF16),
            pltpu.VMEM((SLOTS, BLK, BLK, NLAG), F32),
            pltpu.VMEM((TILES * 64, 2 * COUNTS[2] * PIECE), BF16),
            pltpu.SemaphoreType.DMA((4,)),
            pltpu.SemaphoreType.DMA,
            pltpu.SemaphoreType.DMA((groups,)),
            pltpu.SemaphoreType.DMA,
        ],
        compiler_params=pltpu.CompilerParams(vmem_limit_bytes=60 * 2**20),
    )(plan, late, partial, jnp.asarray(lags[2]))


def solution(mesh):
    return jax.shard_map(
        per_device,
        mesh=mesh,
        in_specs=(P("grp", "dev"), P(), P(), P()),
        out_specs=P(("grp", "dev"), None, None, None),
        check_vma=False,
    )
```

profile of v0, /device:TPU:1, one launch (start us, length us, event | category | flops | bytes accessed | tf_op | source)
XLA Modules:
  0.0 84.6 jit_solution(8915682338435414448)
XLA Ops:
  0.0 79.1 %shard_map.82 = (bf16[2,128,16,128]{3,2,1,0:T(8,128)(2,1)}, bf16[64,8,8,384]{3,2,1,0:T(8,128)(2,1)}, s32[16,128]{1,0:T(8,128)}) custom-call(bf16[960,4096]{1,0:T(8,128)(2,1)} %bitcast.3, bf16[1,64]{1,0:T(2,128)(2,1)} %bitcast.5, s32[2,4160]{1,0:T(2,128)} %bitcast.4, s32[4160]{0:T(1024)} %owner_hbm.1, bf16[832,2048]{1,0:T(8,128)(2,1)} %constant.8.clone.base_ref, ...), custom_call_target="tpu_custom_call" | custom-call | tf_op jit(solution)/shard_map/pallas_call | solution.py:504
  79.2 5.5 %shard_map.83 = f32[64,8,8,384]{3,2,1,0:T(8,128)} custom-call(s32[16,128]{1,0:T(8,128)} %get-tuple-element.8.plan_ref, bf16[2,128,16,128]{3,2,1,0:T(8,128)(2,1)} %get-tuple-element.9.late_ref, bf16[64,8,8,384]{3,2,1,0:T(8,128)(2,1)} %get-tuple-element.10.partial_ref, bf16[512,384]{1,0:T(8,128)(2,1)} %constant.11.clone.lag_ref), custom_call_target="tpu_custom_call" | custom-call | tf_op jit(solution)/shard_map/pallas_call | solution.py:557
where the time goes:
time: 85.8 us; the launch traced here: 84.6 us
  Pallas kernels  84.6 us (99%)
    pallas_call x1, Pallas kernels, per_device(): pl.pallas_call(exchange_kernel, out_shape=(jax.ShapeDtypeStruct((COUNTS[2...  79.1 us
    pallas_call x1, Pallas kernels, per_device(): pl.pallas_call(late_kernel, out_shape=jax.ShapeDtypeStruct((SLOTS, BLK, B...  5.49 us

commit v1 on v0

--- a/solution.py
+++ b/solution.py
@@ -27,8 +27,8 @@
 SLOTS = 64
 PIECE = 128
 PIECES = NF // PIECE
-CUTS = (0, 4, 6, 8)
-COUNTS = (4, 2, 2)
+CUTS = (0, 4, 7, 8)
+COUNTS = (4, 3, 1)
 TILES = 4
 MESH = pl.DeviceIdType.MESH
 F32 = jnp.float32
@@ -274,16 +274,26 @@
             results.append((to_chip, result.astype(BF16)))
         for to_chip, result in results:
             for half in range(2):
-                to = to_chip * 2 + half
-                send[to] = result[:, half * CH : (half + 1) * CH]
-
-                @pl.when(to != dev)
-                def _():
-                    samples_to(to).start()
+                send[to_chip * 2 + half] = result[:, half * CH : (half + 1) * CH]
+
+            @pl.when(to_chip * 2 != dev)
+            def _():
+                samples_to(to_chip * 2).start()
 
         return 0
 
     lax.fori_loop(0, 8, decimate, 0)
+
+    def to_second(step, _):
+        to = chip_at(step * 7 % 16) * 2 + 1
+
+        @pl.when(to != dev)
+        def _():
+            samples_to(to).start()
+
+        return 0
+
+    lax.fori_loop(0, 16, to_second, 0)
     recv[dev] = send[dev]
     for step in range(1, GROUPS):
         pl.semaphore_signal(
@@ -438,11 +448,10 @@
 ):
     count = plan_ref[15, 0]
     pieces = 4
-    size = DEVICES // 2
+    size = DEVICES // pieces
     late_copies = [
         pltpu.make_async_copy(
-            late_ref.at[index // 2, pl.ds(size * (index % 2), size)],
-            late.at[index // 2, pl.ds(size * (index % 2), size)],
+            late_ref.at[:, pl.ds(size * index, size)], late.at[:, pl.ds(size * index, size)],
             late_sem.at[index],
         )
         for index in range(pieces)

time: 85.8 us -> 88.1 us (1.027)
  Pallas kernels: 84.6 us -> 87.1 us
    pallas_call x1, Pallas kernels: 79.1 us -> 81.7 us  [per_device(): pl.pallas_call(exchange_kernel, out_shape=(jax.ShapeDtypeStruct((COUNTS[2...]
where the time goes in v1:
time: 88.1 us; the launch traced here: 87.1 us
  Pallas kernels  87.1 us (99%)
    pallas_call x1, Pallas kernels, per_device(): pl.pallas_call(exchange_kernel, out_shape=(jax.ShapeDtypeStruct((COUNTS[2...  81.7 us
    pallas_call x1, Pallas kernels, per_device(): pl.pallas_call(late_kernel, out_shape=jax.ShapeDtypeStruct((SLOTS, BLK, B...  5.39 us

profile of v1, /device:TPU:1, one launch (start us, length us, event | category | flops | bytes accessed | tf_op | source)
XLA Modules:
  0.0 87.1 jit_solution(8239729553522826902)
XLA Ops:
  0.0 81.7 %shard_map.82 = (bf16[1,128,16,128]{3,2,1,0:T(8,128)(2,1)}, bf16[64,8,8,384]{3,2,1,0:T(8,128)(2,1)}, s32[16,128]{1,0:T(8,128)}) custom-call(bf16[960,4096]{1,0:T(8,128)(2,1)} %bitcast.3, bf16[1,64]{1,0:T(2,128)(2,1)} %bitcast.5, s32[2,4160]{1,0:T(2,128)} %bitcast.4, s32[4160]{0:T(1024)} %owner_hbm.1, bf16[832,2048]{1,0:T(8,128)(2,1)} %constant.8.clone.base_ref, ...), custom_call_target="tpu_custom_call" | custom-call | tf_op jit(solution)/shard_map/pallas_call | solution.py:513
  81.7 5.4 %shard_map.83 = f32[64,8,8,384]{3,2,1,0:T(8,128)} custom-call(s32[16,128]{1,0:T(8,128)} %get-tuple-element.8.plan_ref, bf16[1,128,16,128]{3,2,1,0:T(8,128)(2,1)} %get-tuple-element.9.late_ref, bf16[64,8,8,384]{3,2,1,0:T(8,128)(2,1)} %get-tuple-element.10.partial_ref, bf16[256,384]{1,0:T(8,128)(2,1)} %constant.11.clone.lag_ref), custom_call_target="tpu_custom_call" | custom-call | tf_op jit(solution)/shard_map/pallas_call | solution.py:566

commit v2 on v0

--- a/solution.py
+++ b/solution.py
@@ -22,13 +22,15 @@
 DEVICES = 128
 COLS = NT // MEMBERS
 EXT = 208
+USED = 205
+RANK = 96
 PARTS = 8
 CH = 128
 SLOTS = 64
 PIECE = 128
 PIECES = NF // PIECE
-CUTS = (0, 4, 6, 8)
-COUNTS = (4, 2, 2)
+CUTS = (0, 4, 7, 8)
+COUNTS = (4, 3, 1)
 TILES = 4
 MESH = pl.DeviceIdType.MESH
 F32 = jnp.float32
@@ -41,11 +43,27 @@
     return np.cos(angle) * factor, -np.sin(angle) * factor
 
 
-def base_table():
-    rows = (np.arange(4)[:, None] * COLS + np.arange(EXT)[None, :]).reshape(-1)
-    phase = rows[:, None] * (F0 + np.arange(NF))[None, :] % NT
-    real, imag = trig(phase)
-    return np.concatenate([real, imag], axis=1).astype(ml_dtypes.bfloat16)
+def base_tables():
+    samples = np.arange(USED)
+    width = (F0 + NF) / NT
+    steps = samples[1:] * (USED - samples[1:]) / 2
+    diagonal = ((USED - 1) / 2 - samples) ** 2 * math.cos(2 * math.pi * width)
+    _, vectors = np.linalg.eigh(np.diag(diagonal) + np.diag(steps, 1) + np.diag(steps, -1))
+    basis = vectors[:, ::-1][:, :RANK].T
+    half = basis[:, : USED // 2]
+    basis = basis * np.sign(np.take_along_axis(half, np.abs(half).argmax(axis=1)[:, None], axis=1))
+
+    def table(place):
+        rows = place * COLS + samples
+        angle = 2.0 * math.pi / NT * (rows[:, None] * (F0 + np.arange(NF))[None, :] % NT)
+        return np.concatenate([np.cos(angle), -np.sin(angle)], axis=1)
+
+    assert np.abs(basis.T @ (basis @ table(0)) - table(0)).max() < 1e-10
+    rows = np.concatenate([basis @ table(place) for place in range(4)], axis=0)
+    basis = np.pad(basis, ((0, 0), (0, EXT - USED)))
+    high = basis.astype(ml_dtypes.bfloat16)
+    low = (basis - high.astype(np.float64)).astype(ml_dtypes.bfloat16)
+    return np.concatenate([high, low], axis=0), rows.astype(ml_dtypes.bfloat16)
 
 
 def turns(part):
@@ -90,7 +108,7 @@
         [pltpu.roll(first_rows, 8 * DECIM * index, 1) for index in range(EXT // 8)], axis=0
     )
     row = lax.broadcasted_iota(jnp.int32, (EXT, 1024), 0)
-    limit = jnp.where(member == MEMBERS - 1, COLS, 205)
+    limit = jnp.where(member == MEMBERS - 1, COLS, USED)
     return jnp.where(row < limit, band, 0.0)[:, :960].astype(BF16)
 
 
@@ -191,9 +209,9 @@
 
 
 def exchange_kernel(
-    strain_ref, taps_hbm, tiles_hbm, owner_hbm, base_ref, lag0_ref, lag1_ref,
+    strain_ref, taps_hbm, tiles_hbm, owner_hbm, basis_hbm, base_ref, lag0_ref, lag1_ref,
     late_ref, partial_ref, plan_out_ref,
-    raw, taps_ref, tiles_ref, owner_ref, base, lag0, lag1, band, plan_vector, plan, send, recv, acc,
+    raw, taps_ref, tiles_ref, owner_ref, basis, base, lag0, lag1, band, plan_vector, plan, send, recv, acc,
     gathered0, gathered1, gathered2, gathered3, gathered4, gathered5, gathered6, gathered7,
     out0, out1, out2, in0, in1, cross0, cross1, first_sums, partial,
     raw_sem, small_sem, base_sem, lag_sem, plan_sem, plan_out_sem, send_sem, recv_sem,
@@ -224,7 +242,8 @@
         raw_copy(step * 7 % 16).start()
         return 0
 
-    small = ((taps_hbm, taps_ref), (tiles_hbm, tiles_ref), (owner_hbm, owner_ref))
+    small = ((taps_hbm, taps_ref), (basis_hbm, basis), (tiles_hbm, tiles_ref))
+    small = small + ((owner_hbm, owner_ref),)
     small_copies = [
         pltpu.make_async_copy(source, into, small_sem.at[index])
         for index, (source, into) in enumerate(small)
@@ -255,6 +274,7 @@
             barrier, inc=1, device_id=((grp + step) % GROUPS, dev), device_id_type=MESH
         )
     small_copies[0].wait()
+    small_copies[1].wait()
     band[...] = make_band(dev, taps_ref[...])
     pl.semaphore_wait(barrier, MEMBERS - 1 + GROUPS - 1)
 
@@ -270,12 +290,13 @@
             offset = (pair * 2 + index) * 7 % 16
             raw_copy(offset).wait()
             to_chip = chip_at(offset)
-            result = jnp.dot(band[...], raw[to_chip], preferred_element_type=F32)
-            results.append((to_chip, result.astype(BF16)))
+            result = jnp.dot(band[...], raw[to_chip], preferred_element_type=F32).astype(BF16)
+            halves = jnp.dot(basis[...], result, preferred_element_type=F32)
+            results.append((to_chip, (halves[:RANK] + halves[RANK:]).astype(BF16)))
         for to_chip, result in results:
             for half in range(2):
+                send[to_chip * 2 + half] = result[:, half * CH : (half + 1) * CH]
                 to = to_chip * 2 + half
-                send[to] = result[:, half * CH : (half + 1) * CH]
 
                 @pl.when(to != dev)
                 def _():
@@ -289,7 +310,7 @@
         pl.semaphore_signal(
             plane_sem, inc=1, device_id=((grp + step) % GROUPS, dev), device_id_type=MESH
         )
-    for copy in small_copies[1:]:
+    for copy in small_copies[2:]:
         copy.wait()
     tile_rows = [stack_rows([tiles_ref[side : side + 1, :]], 40, 0) for side in range(2)]
     owner_rows = stack_rows([owner_ref[...].reshape(1, -1)], 40, -1)
@@ -315,10 +336,10 @@
                     device_id=(grp, source), device_id_type=MESH,
                 ).wait_recv()
 
-        samples = recv[pl.ds(from_chip * 2, 2)].reshape(2 * EXT, CH)
+        samples = recv[pl.ds(from_chip * 2, 2)].reshape(2 * RANK, CH)
         part = from_chip // 2
         cosine, sine = turns(part)
-        table = base[pl.ds(pl.multiple_of(from_chip % 2 * (2 * EXT), 2 * EXT), 2 * EXT), :]
+        table = base[pl.ds(pl.multiple_of(from_chip % 2 * (2 * RANK), 2 * RANK), 2 * RANK), :]
         result = lax.dot_general(
             samples, table, (((0,), (0,)), ((), ())), preferred_element_type=F32
         )
@@ -438,11 +459,10 @@
 ):
     count = plan_ref[15, 0]
     pieces = 4
-    size = DEVICES // 2
+    size = DEVICES // pieces
     late_copies = [
         pltpu.make_async_copy(
-            late_ref.at[index // 2, pl.ds(size * (index % 2), size)],
-            late.at[index // 2, pl.ds(size * (index % 2), size)],
+            late_ref.at[:, pl.ds(size * index, size)], late.at[:, pl.ds(size * index, size)],
             late_sem.at[index],
         )
         for index in range(pieces)
@@ -496,6 +516,7 @@
 def per_device(strain, taps, tiles, owner):
     hbm = pl.BlockSpec(memory_space=pl.ANY)
     lag = lag_table()
+    basis, rows = base_tables()
     lags = [
         lag.reshape(2, PIECES, PIECE, NLAG)[:, CUTS[part] : CUTS[part + 1]].reshape(-1, NLAG)
         for part in range(3)
@@ -508,21 +529,22 @@
             jax.ShapeDtypeStruct((SLOTS, BLK, BLK, NLAG), BF16),
             jax.ShapeDtypeStruct((16, 128), jnp.int32),
         ),
-        in_specs=[hbm] * 7,
+        in_specs=[hbm] * 8,
         out_specs=(hbm, hbm, hbm),
         scratch_shapes=[
             pltpu.VMEM((16, 960, 256), BF16),
             pltpu.VMEM((1, NTAP), BF16),
             pltpu.VMEM((2, 4160), jnp.int32),
             pltpu.VMEM((4160,), jnp.int32),
-            pltpu.VMEM((4 * EXT, 2 * NF), BF16),
+            pltpu.VMEM((2 * RANK, EXT), BF16),
+            pltpu.VMEM((4 * RANK, 2 * NF), BF16),
             pltpu.VMEM((2 * COUNTS[0] * PIECE, NLAG), BF16),
             pltpu.VMEM((2 * COUNTS[1] * PIECE, NLAG), BF16),
             pltpu.VMEM((EXT, 960), BF16),
             pltpu.VMEM((16, 128), jnp.int32),
             pltpu.SMEM((16, 128), jnp.int32),
-            pltpu.VMEM((MEMBERS, EXT, CH), BF16),
-            pltpu.VMEM((MEMBERS, EXT, CH), BF16),
+            pltpu.VMEM((MEMBERS, RANK, CH), BF16),
+            pltpu.VMEM((MEMBERS, RANK, CH), BF16),
             pltpu.VMEM((CH, 2 * NF), F32),
             *[pltpu.VMEM((4, 16, 2 * BLK, PIECE), BF16) for _ in range(PIECES)],
             *[pltpu.VMEM((count, MEMBERS, 4, 2 * BLK, PIECE), BF16) for count in COUNTS],
@@ -531,7 +553,7 @@
             pltpu.VMEM((SLOTS, BLK, BLK, NLAG), F32),
             pltpu.VMEM((SLOTS, BLK, BLK, NLAG), BF16),
             pltpu.SemaphoreType.DMA((16,)),
-            pltpu.SemaphoreType.DMA((3,)),
+            pltpu.SemaphoreType.DMA((4,)),
             pltpu.SemaphoreType.DMA,
             pltpu.SemaphoreType.DMA((2,)),
             pltpu.SemaphoreType.DMA,
@@ -550,7 +572,7 @@
             collective_id=0, has_side_effects=True, vmem_limit_bytes=60 * 2**20
         ),
     )(
-        strain.T, taps[None, :], tiles.T, owner, jnp.asarray(base_table()),
+        strain.T, taps[None, :], tiles.T, owner, jnp.asarray(basis), jnp.asarray(rows),
         jnp.asarray(lags[0]), jnp.asarray(lags[1]),
     )
 

time: 85.8 us -> 85.4 us (level); the launches traced: 84.6 us -> 85.2 us
  no operation moved by 1% of the time
where the time goes in v2:
time: 85.4 us; the launch traced here: 85.2 us
  Pallas kernels  85.2 us (100%)
    pallas_call x1, Pallas kernels, per_device(): pl.pallas_call(exchange_kernel, out_shape=(jax.ShapeDtypeStruct((COUNTS[2...  79.5 us
    pallas_call x1, Pallas kernels, per_device(): pl.pallas_call(late_kernel, out_shape=jax.ShapeDtypeStruct((SLOTS, BLK, B...  5.7 us

profile of v2, /device:TPU:1, one launch (start us, length us, event | category | flops | bytes accessed | tf_op | source)
XLA Modules:
  0.0 85.2 jit_solution(4540380240277644135)
XLA Ops:
  0.0 79.5 %shard_map.91 = (bf16[1,128,16,128]{3,2,1,0:T(8,128)(2,1)}, bf16[64,8,8,384]{3,2,1,0:T(8,128)(2,1)}, s32[16,128]{1,0:T(8,128)}) custom-call(bf16[960,4096]{1,0:T(8,128)(2,1)} %bitcast.3, bf16[1,64]{1,0:T(2,128)(2,1)} %bitcast.5, s32[2,4160]{1,0:T(2,128)} %bitcast.4, s32[4160]{0:T(1024)} %owner_hbm.1, bf16[192,208]{1,0:T(8,128)(2,1)} %constant.10.clone.basis_hbm, ...), custom_call_target="tpu_custom_call" | custom-call | tf_op jit(solution)/shard_map/pallas_call | solution.py:525
  79.5 5.7 %shard_map.92 = f32[64,8,8,384]{3,2,1,0:T(8,128)} custom-call(s32[16,128]{1,0:T(8,128)} %get-tuple-element.8.plan_ref, bf16[1,128,16,128]{3,2,1,0:T(8,128)(2,1)} %get-tuple-element.9.late_ref, bf16[64,8,8,384]{3,2,1,0:T(8,128)(2,1)} %get-tuple-element.10.partial_ref, bf16[256,384]{1,0:T(8,128)(2,1)} %constant.14.clone.lag_ref), custom_call_target="tpu_custom_call" | custom-call | tf_op jit(solution)/shard_map/pallas_call | solution.py:579

commit v3 on v2

--- a/solution.py
+++ b/solution.py
@@ -29,8 +29,9 @@
 SLOTS = 64
 PIECE = 128
 PIECES = NF // PIECE
-CUTS = (0, 4, 7, 8)
-COUNTS = (4, 3, 1)
+CUTS = (0, 4, 6, 7, 8)
+COUNTS = (4, 2, 1, 1)
+EARLY = len(COUNTS) - 1
 TILES = 4
 MESH = pl.DeviceIdType.MESH
 F32 = jnp.float32
@@ -59,22 +60,11 @@
         return np.concatenate([np.cos(angle), -np.sin(angle)], axis=1)
 
     assert np.abs(basis.T @ (basis @ table(0)) - table(0)).max() < 1e-10
-    rows = np.concatenate([basis @ table(place) for place in range(4)], axis=0)
+    rows = np.concatenate([basis @ table(place) for place in range(MEMBERS)], axis=0)
     basis = np.pad(basis, ((0, 0), (0, EXT - USED)))
     high = basis.astype(ml_dtypes.bfloat16)
     low = (basis - high.astype(np.float64)).astype(ml_dtypes.bfloat16)
     return np.concatenate([high, low], axis=0), rows.astype(ml_dtypes.bfloat16)
-
-
-def turns(part):
-    eighth = part * lax.broadcasted_iota(jnp.int32, (1, NF), 1) % 8
-    half = math.sqrt(0.5)
-
-    def wave(eighth):
-        size = jnp.where(eighth % 4 == 0, 1.0, jnp.where(eighth % 4 == 2, 0.0, half))
-        return jnp.where((eighth >= 3) & (eighth <= 5), -size, size)
-
-    return wave(eighth), wave((eighth + 6) % 8)
 
 
 def lag_table():
@@ -209,11 +199,11 @@
 
 
 def exchange_kernel(
-    strain_ref, taps_hbm, tiles_hbm, owner_hbm, basis_hbm, base_ref, lag0_ref, lag1_ref,
+    strain_ref, taps_hbm, tiles_hbm, owner_hbm, basis_hbm, base_ref, lag0_ref, lag1_ref, lag2_ref,
     late_ref, partial_ref, plan_out_ref,
-    raw, taps_ref, tiles_ref, owner_ref, basis, base, lag0, lag1, band, plan_vector, plan, send, recv, acc,
+    raw, taps_ref, tiles_ref, owner_ref, basis, base, lag0, lag1, lag2, band, plan_vector, plan, send, recv, acc,
     gathered0, gathered1, gathered2, gathered3, gathered4, gathered5, gathered6, gathered7,
-    out0, out1, out2, in0, in1, cross0, cross1, first_sums, partial,
+    out0, out1, out2, out3, in0, in1, in2, cross0, cross1, cross2, first_sums, partial,
     raw_sem, small_sem, base_sem, lag_sem, plan_sem, plan_out_sem, send_sem, recv_sem,
     line_sem, gather_sem, out_sem, in_sem, own_sem, partial_sem, plane_sem,
 ):
@@ -256,6 +246,7 @@
     lag_copies = [
         pltpu.make_async_copy(lag0_ref, lag0, lag_sem.at[0]),
         pltpu.make_async_copy(lag1_ref, lag1, lag_sem.at[1]),
+        pltpu.make_async_copy(lag2_ref, lag2, lag_sem.at[2]),
     ]
     for copy in lag_copies:
         copy.start()
@@ -310,23 +301,14 @@
         pl.semaphore_signal(
             plane_sem, inc=1, device_id=((grp + step) % GROUPS, dev), device_id_type=MESH
         )
-    for copy in small_copies[2:]:
-        copy.wait()
-    tile_rows = [stack_rows([tiles_ref[side : side + 1, :]], 40, 0) for side in range(2)]
-    owner_rows = stack_rows([owner_ref[...].reshape(1, -1)], 40, -1)
-    make_plan(me, *tile_rows, owner_rows, plan_vector)
-    plan_copy = pltpu.make_async_copy(plan_vector, plan, plan_sem)
-    plan_copy.start()
-    plan_out = pltpu.make_async_copy(plan_vector, plan_out_ref, plan_out_sem)
-    plan_out.start()
     base_copy.wait()
     acc[...] = jnp.zeros_like(acc)
 
     def transform(step, _):
-        offset = step * 7 % 16
-        from_chip = (zc - offset // 4 + 4) % 4 * 4 + (xc - offset % 4 + 4) % 4
-        for half in range(2):
-            source = from_chip * 2 + half
+        plane = (zc + step) % 4
+        first = plane * 8
+        for index in range(8):
+            source = first + index
 
             @pl.when(source != dev)
             def _():
@@ -336,19 +318,13 @@
                     device_id=(grp, source), device_id_type=MESH,
                 ).wait_recv()
 
-        samples = recv[pl.ds(from_chip * 2, 2)].reshape(2 * RANK, CH)
-        part = from_chip // 2
-        cosine, sine = turns(part)
-        table = base[pl.ds(pl.multiple_of(from_chip % 2 * (2 * RANK), 2 * RANK), 2 * RANK), :]
-        result = lax.dot_general(
-            samples, table, (((0,), (0,)), ((), ())), preferred_element_type=F32
-        )
-        real, imag = result[:, :NF], result[:, NF:]
-        acc[:, :NF] += real * cosine + imag * sine
-        acc[:, NF:] += imag * cosine - real * sine
-        return 0
-
-    lax.fori_loop(0, 16, transform, 0)
+        samples = recv[pl.ds(first, 8)].reshape(8 * RANK, CH)
+        acc[...] += lax.dot_general(
+            samples, base[plane], (((0,), (0,)), ((), ())), preferred_element_type=F32
+        )
+        return 0
+
+    lax.fori_loop(0, 4, transform, 0)
 
     real, imag = acc[:, :NF], acc[:, NF:]
     power = real * real + imag * imag
@@ -357,7 +333,8 @@
     whitened = jnp.concatenate(
         [(real * scale).reshape(16, BLK, NF), (imag * scale).reshape(16, BLK, NF)], axis=1
     ).astype(BF16)
-    outs, ins = (out0, out1, out2), (in0, in1, late_ref)
+    outs, ins = (out0, out1, out2, out3), (in0, in1, in2, late_ref)
+    crosses, lags = (cross0, cross1, cross2), (lag0, lag1, lag2)
     gathered = (gathered0, gathered1, gathered2, gathered3)
     gathered = gathered + (gathered4, gathered5, gathered6, gathered7)
     pl.semaphore_wait(plane_sem, GROUPS - 1)
@@ -400,9 +377,18 @@
             outs[part].at[index, 0], ins[part].at[index, pl.ds(line * 4, 4)], own_sem.at[piece]
         )
 
+    for copy in small_copies[2:]:
+        copy.wait()
+    tile_rows = [stack_rows([tiles_ref[side : side + 1, :]], 40, 0) for side in range(2)]
+    owner_rows = stack_rows([owner_ref[...].reshape(1, -1)], 40, -1)
+    make_plan(me, *tile_rows, owner_rows, plan_vector)
+    plan_copy = pltpu.make_async_copy(plan_vector, plan, plan_sem)
+    plan_copy.start()
+    plan_out = pltpu.make_async_copy(plan_vector, plan_out_ref, plan_out_sem)
+    plan_out.start()
     plan_copy.wait()
     own_copies = []
-    for part in range(3):
+    for part in range(EARLY + 1):
         for piece in range(CUTS[part], CUTS[part + 1]):
             others = gathered[piece].at[pl.ds(0, 3)]
             pltpu.make_async_copy(others, others, gather_sem.at[piece]).wait()
@@ -420,34 +406,35 @@
         others = ins[part].at[:, pl.ds(0, DEVICES - 4)]
         pltpu.make_async_copy(others, others, in_sem.at[part]).wait()
 
-    def lagged_tiles(group, into, cross, lag, part):
-        for tile in range(TILES):
-            cross_spectra(into, plan, cross, group * TILES + tile, tile, axes_of(part))
-        lagged = jnp.dot(cross[...], lag[...], preferred_element_type=F32)
-        return lagged.reshape(TILES, BLK, BLK, NLAG)
-
-    def first_tiles(group, _):
-        first_sums[pl.ds(group * TILES, TILES)] = lagged_tiles(group, in0, cross0, lag0, 0)
-        return 0
-
-    def second_tiles(group, _):
-        rows = pl.ds(group * TILES, TILES)
-        partial[rows] = (first_sums[rows] + lagged_tiles(group, in1, cross1, lag1, 1)).astype(BF16)
-        pltpu.make_async_copy(partial.at[rows], partial_ref.at[rows], partial_sem).start()
-        return 0
+    def tiles_of(part):
+        def one(group, _):
+            for tile in range(TILES):
+                cross_spectra(ins[part], plan, crosses[part], group * TILES + tile, tile, axes_of(part))
+            lagged = jnp.dot(crosses[part][...], lags[part][...], preferred_element_type=F32)
+            lagged = lagged.reshape(TILES, BLK, BLK, NLAG)
+            rows = pl.ds(group * TILES, TILES)
+            if part > 0:
+                lagged = lagged + first_sums[rows]
+            if part < EARLY - 1:
+                first_sums[rows] = lagged
+            else:
+                partial[rows] = lagged.astype(BF16)
+                pltpu.make_async_copy(partial.at[rows], partial_ref.at[rows], partial_sem).start()
+            return 0
+
+        lax.fori_loop(0, SLOTS // TILES, one, 0)
 
     for copy in lag_copies:
         copy.wait()
-    await_part(0)
-    lax.fori_loop(0, SLOTS // TILES, first_tiles, 0)
-    await_part(1)
-    lax.fori_loop(0, SLOTS // TILES, second_tiles, 0)
+    for part in range(EARLY):
+        await_part(part)
+        tiles_of(part)
     pltpu.make_async_copy(partial, partial_ref, partial_sem).wait()
     plan_out.wait()
-    for part in range(3):
+    for part in range(EARLY + 1):
         sent = outs[part].at[:, pl.ds(0, MEMBERS - 1)]
         pltpu.make_async_copy(sent, sent, out_sem.at[part]).wait()
-    await_part(2)
+    await_part(EARLY)
     for piece in range(PIECES):
         others = gathered[piece].at[pl.ds(0, 3)]
         pltpu.make_async_copy(others, others, line_sem.at[piece]).wait()
@@ -496,7 +483,7 @@
         @pl.when(group * TILES < count)
         def _():
             for tile in range(TILES):
-                cross_spectra(late, plan_ref, cross, group * TILES + tile, tile, axes_of(2))
+                cross_spectra(late, plan_ref, cross, group * TILES + tile, tile, axes_of(EARLY))
             lagged = jnp.dot(cross[...], lag[...], preferred_element_type=F32)
             lagged = lagged + partial[rows(group)].astype(F32).reshape(lagged.shape)
             index = lax.broadcasted_iota(jnp.int32, lagged.shape, 0) // 64 + group * TILES
@@ -519,17 +506,17 @@
     basis, rows = base_tables()
     lags = [
         lag.reshape(2, PIECES, PIECE, NLAG)[:, CUTS[part] : CUTS[part + 1]].reshape(-1, NLAG)
-        for part in range(3)
+        for part in range(EARLY + 1)
     ]
     groups = SLOTS // TILES
     late, partial, plan = pl.pallas_call(
         exchange_kernel,
         out_shape=(
-            jax.ShapeDtypeStruct((COUNTS[2], DEVICES, 2 * BLK, PIECE), BF16),
+            jax.ShapeDtypeStruct((COUNTS[EARLY], DEVICES, 2 * BLK, PIECE), BF16),
             jax.ShapeDtypeStruct((SLOTS, BLK, BLK, NLAG), BF16),
             jax.ShapeDtypeStruct((16, 128), jnp.int32),
         ),
-        in_specs=[hbm] * 8,
+        in_specs=[hbm] * (6 + EARLY),
         out_specs=(hbm, hbm, hbm),
         scratch_shapes=[
             pltpu.VMEM((16, 960, 256), BF16),
@@ -537,9 +524,8 @@
             pltpu.VMEM((2, 4160), jnp.int32),
             pltpu.VMEM((4160,), jnp.int32),
             pltpu.VMEM((2 * RANK, EXT), BF16),
-            pltpu.VMEM((4 * RANK, 2 * NF), BF16),
-            pltpu.VMEM((2 * COUNTS[0] * PIECE, NLAG), BF16),
-            pltpu.VMEM((2 * COUNTS[1] * PIECE, NLAG), BF16),
+            pltpu.VMEM((4, 8 * RANK, 2 * NF), BF16),
+            *[pltpu.VMEM((2 * count * PIECE, NLAG), BF16) for count in COUNTS[:EARLY]],
             pltpu.VMEM((EXT, 960), BF16),
             pltpu.VMEM((16, 128), jnp.int32),
             pltpu.SMEM((16, 128), jnp.int32),
@@ -548,22 +534,22 @@
             pltpu.VMEM((CH, 2 * NF), F32),
             *[pltpu.VMEM((4, 16, 2 * BLK, PIECE), BF16) for _ in range(PIECES)],
             *[pltpu.VMEM((count, MEMBERS, 4, 2 * BLK, PIECE), BF16) for count in COUNTS],
-            *[pltpu.VMEM((count, DEVICES, 2 * BLK, PIECE), BF16) for count in COUNTS[:2]],
-            *[pltpu.VMEM((TILES * 64, 2 * count * PIECE), BF16) for count in COUNTS[:2]],
+            *[pltpu.VMEM((count, DEVICES, 2 * BLK, PIECE), BF16) for count in COUNTS[:EARLY]],
+            *[pltpu.VMEM((TILES * 64, 2 * count * PIECE), BF16) for count in COUNTS[:EARLY]],
             pltpu.VMEM((SLOTS, BLK, BLK, NLAG), F32),
             pltpu.VMEM((SLOTS, BLK, BLK, NLAG), BF16),
             pltpu.SemaphoreType.DMA((16,)),
             pltpu.SemaphoreType.DMA((4,)),
             pltpu.SemaphoreType.DMA,
-            pltpu.SemaphoreType.DMA((2,)),
+            pltpu.SemaphoreType.DMA((EARLY,)),
             pltpu.SemaphoreType.DMA,
             pltpu.SemaphoreType.DMA,
             pltpu.SemaphoreType.DMA((MEMBERS,)),
             pltpu.SemaphoreType.DMA((MEMBERS,)),
             pltpu.SemaphoreType.DMA((PIECES,)),
             pltpu.SemaphoreType.DMA((PIECES,)),
-            pltpu.SemaphoreType.DMA((3,)),
-            pltpu.SemaphoreType.DMA((3,)),
+            pltpu.SemaphoreType.DMA((EARLY + 1,)),
+            pltpu.SemaphoreType.DMA((EARLY + 1,)),
             pltpu.SemaphoreType.DMA((PIECES,)),
             pltpu.SemaphoreType.DMA,
             pltpu.SemaphoreType.REGULAR,
@@ -572,8 +558,8 @@
             collective_id=0, has_side_effects=True, vmem_limit_bytes=60 * 2**20
         ),
     )(
-        strain.T, taps[None, :], tiles.T, owner, jnp.asarray(basis), jnp.asarray(rows),
-        jnp.asarray(lags[0]), jnp.asarray(lags[1]),
+        strain.T, taps[None, :], tiles.T, owner, jnp.asarray(basis), jnp.asarray(rows.reshape(4, 8 * RANK, 2 * NF)),
+        *[jnp.asarray(part) for part in lags[:EARLY]],
     )
 
     return pl.pallas_call(
@@ -582,18 +568,18 @@
         in_specs=[pl.BlockSpec(memory_space=pltpu.SMEM), hbm, hbm, hbm],
         out_specs=hbm,
         scratch_shapes=[
-            pltpu.VMEM((COUNTS[2], DEVICES, 2 * BLK, PIECE), BF16),
-            pltpu.VMEM((2 * COUNTS[2] * PIECE, NLAG), BF16),
+            pltpu.VMEM((COUNTS[EARLY], DEVICES, 2 * BLK, PIECE), BF16),
+            pltpu.VMEM((2 * COUNTS[EARLY] * PIECE, NLAG), BF16),
             pltpu.VMEM((SLOTS, BLK, BLK, NLAG), BF16),
             pltpu.VMEM((SLOTS, BLK, BLK, NLAG), F32),
-            pltpu.VMEM((TILES * 64, 2 * COUNTS[2] * PIECE), BF16),
+            pltpu.VMEM((TILES * 64, 2 * COUNTS[EARLY] * PIECE), BF16),
             pltpu.SemaphoreType.DMA((4,)),
             pltpu.SemaphoreType.DMA,
             pltpu.SemaphoreType.DMA((groups,)),
             pltpu.SemaphoreType.DMA,
         ],
         compiler_params=pltpu.CompilerParams(vmem_limit_bytes=60 * 2**20),
-    )(plan, late, partial, jnp.asarray(lags[2]))
+    )(plan, late, partial, jnp.asarray(lags[EARLY]))
 
 
 def solution(mesh):

time: 85.4 us -> 77.9 us (0.912)
  Pallas kernels: 85.2 us -> 77.7 us
    pallas_call x1, Pallas kernels: 79.5 us -> 72 us  [per_device(): pl.pallas_call(exchange_kernel, out_shape=(jax.ShapeDtypeStruct((COUNTS[E...]
where the time goes in v3:
time: 77.9 us; the launch traced here: 77.7 us
  Pallas kernels  77.7 us (100%)
    pallas_call x1, Pallas kernels, per_device(): pl.pallas_call(exchange_kernel, out_shape=(jax.ShapeDtypeStruct((COUNTS[E...  72 us
    pallas_call x1, Pallas kernels, per_device(): pl.pallas_call(late_kernel, out_shape=jax.ShapeDtypeStruct((SLOTS, BLK, B...  5.69 us

profile of v3, /device:TPU:1, one launch (start us, length us, event | category | flops | bytes accessed | tf_op | source)
XLA Modules:
  0.0 77.7 jit_solution(1568154742340108822)
XLA Ops:
  0.0 72.0 %shard_map.100 = (bf16[1,128,16,128]{3,2,1,0:T(8,128)(2,1)}, bf16[64,8,8,384]{3,2,1,0:T(8,128)(2,1)}, s32[16,128]{1,0:T(8,128)}) custom-call(bf16[960,4096]{1,0:T(8,128)(2,1)} %bitcast.3, bf16[1,64]{1,0:T(2,128)(2,1)} %bitcast.5, s32[2,4160]{1,0:T(2,128)} %bitcast.4, s32[4160]{0:T(1024)} %owner_hbm.1, bf16[192,208]{1,0:T(8,128)(2,1)} %constant.12.clone.basis_hbm, ...), custom_call_target="tpu_custom_call" | custom-call | tf_op jit(solution)/shard_map/pallas_call | solution.py:512
  72.0 5.7 %shard_map.101 = f32[64,8,8,384]{3,2,1,0:T(8,128)} custom-call(s32[16,128]{1,0:T(8,128)} %get-tuple-element.8.plan_ref, bf16[1,128,16,128]{3,2,1,0:T(8,128)(2,1)} %get-tuple-element.9.late_ref, bf16[64,8,8,384]{3,2,1,0:T(8,128)(2,1)} %get-tuple-element.10.partial_ref, bf16[256,384]{1,0:T(8,128)(2,1)} %constant.17.clone.lag_ref), custom_call_target="tpu_custom_call" | custom-call | tf_op jit(solution)/shard_map/pallas_call | solution.py:565

commit v4 on v3

--- a/solution.py
+++ b/solution.py
@@ -24,6 +24,7 @@
 EXT = 208
 USED = 205
 RANK = 96
+STRETCHES = ((0, 64), (48, 120), (96, 168), (144, 208))
 PARTS = 8
 CH = 128
 SLOTS = 64
@@ -100,6 +101,28 @@
     row = lax.broadcasted_iota(jnp.int32, (EXT, 1024), 0)
     limit = jnp.where(member == MEMBERS - 1, COLS, USED)
     return jnp.where(row < limit, band, 0.0)[:, :960].astype(BF16)
+
+
+def filtered(band, raw):
+    count = raw.shape[0]
+    sums = [
+        jnp.dot(
+            band[low:high, 256 * index : min(256 * (index + 1), count)],
+            raw[256 * index : min(256 * (index + 1), count)],
+            preferred_element_type=F32,
+        )
+        for index, (low, high) in enumerate(STRETCHES)
+    ]
+    pieces = []
+    done = 0
+    for index, (low, high) in enumerate(STRETCHES):
+        end = STRETCHES[index + 1][0] if index + 1 < len(STRETCHES) else high
+        pieces.append(sums[index][done - low : end - low])
+        if end < high:
+            after = STRETCHES[index + 1][0]
+            pieces.append(sums[index][end - low :] + sums[index + 1][: high - after])
+        done = high
+    return jnp.concatenate(pieces, axis=0)
 
 
 def coordinates(device):
@@ -241,15 +264,14 @@
     for copy in small_copies:
         copy.start()
     lax.fori_loop(0, 16, fetch, 0)
-    base_copy = pltpu.make_async_copy(base_ref, base, base_sem)
-    base_copy.start()
+    def base_copy(plane):
+        return pltpu.make_async_copy(base_ref.at[plane], base.at[plane], base_sem.at[plane])
+
     lag_copies = [
         pltpu.make_async_copy(lag0_ref, lag0, lag_sem.at[0]),
         pltpu.make_async_copy(lag1_ref, lag1, lag_sem.at[1]),
         pltpu.make_async_copy(lag2_ref, lag2, lag_sem.at[2]),
     ]
-    for copy in lag_copies:
-        copy.start()
 
     barrier = pltpu.get_barrier_semaphore()
 
@@ -281,9 +303,13 @@
             offset = (pair * 2 + index) * 7 % 16
             raw_copy(offset).wait()
             to_chip = chip_at(offset)
-            result = jnp.dot(band[...], raw[to_chip], preferred_element_type=F32).astype(BF16)
+            result = filtered(band, raw.at[to_chip]).astype(BF16)
             halves = jnp.dot(basis[...], result, preferred_element_type=F32)
             results.append((to_chip, (halves[:RANK] + halves[RANK:]).astype(BF16)))
+        @pl.when(pair % 2 == 1)
+        def _():
+            base_copy((zc + pair // 2) % 4).start()
+
         for to_chip, result in results:
             for half in range(2):
                 send[to_chip * 2 + half] = result[:, half * CH : (half + 1) * CH]
@@ -296,12 +322,13 @@
         return 0
 
     lax.fori_loop(0, 8, decimate, 0)
+    for copy in lag_copies:
+        copy.start()
     recv[dev] = send[dev]
     for step in range(1, GROUPS):
         pl.semaphore_signal(
             plane_sem, inc=1, device_id=((grp + step) % GROUPS, dev), device_id_type=MESH
         )
-    base_copy.wait()
     acc[...] = jnp.zeros_like(acc)
 
     def transform(step, _):
@@ -318,6 +345,7 @@
                     device_id=(grp, source), device_id_type=MESH,
                 ).wait_recv()
 
+        base_copy(plane).wait()
         samples = recv[pl.ds(first, 8)].reshape(8 * RANK, CH)
         acc[...] += lax.dot_general(
             samples, base[plane], (((0,), (0,)), ((), ())), preferred_element_type=F32
@@ -330,9 +358,6 @@
     power = real * real + imag * imag
     level = jnp.mean(power, axis=1, keepdims=True)
     scale = lax.rsqrt(power + level + 1e-06)
-    whitened = jnp.concatenate(
-        [(real * scale).reshape(16, BLK, NF), (imag * scale).reshape(16, BLK, NF)], axis=1
-    ).astype(BF16)
     outs, ins = (out0, out1, out2, out3), (in0, in1, in2, late_ref)
     crosses, lags = (cross0, cross1, cross2), (lag0, lag1, lag2)
     gathered = (gathered0, gathered1, gathered2, gathered3)
@@ -340,7 +365,12 @@
     pl.semaphore_wait(plane_sem, GROUPS - 1)
     for piece in range(PIECES):
         line, place = line_and_place(me, piece % 3)
-        gathered[piece][place] = whitened[:, :, piece * PIECE : (piece + 1) * PIECE]
+        bins = slice(piece * PIECE, (piece + 1) * PIECE)
+        factor = scale[:, bins]
+        parts = (acc[:, bins] * factor, acc[:, NF + piece * PIECE : NF + (piece + 1) * PIECE] * factor)
+        gathered[piece][place] = jnp.concatenate(
+            [half.reshape(16, BLK, PIECE) for half in parts], axis=1
+        ).astype(BF16)
         for step in (1, 3, 2):
             to = device_of(line, (place + step) % 4, piece % 3)
             pltpu.make_async_remote_copy(
@@ -540,7 +570,7 @@
             pltpu.VMEM((SLOTS, BLK, BLK, NLAG), BF16),
             pltpu.SemaphoreType.DMA((16,)),
             pltpu.SemaphoreType.DMA((4,)),
-            pltpu.SemaphoreType.DMA,
+            pltpu.SemaphoreType.DMA((4,)),
             pltpu.SemaphoreType.DMA((EARLY,)),
             pltpu.SemaphoreType.DMA,
             pltpu.SemaphoreType.DMA,

time: 77.9 us -> 77.3 us (level)
  no operation moved by 1% of the time
where the time goes in v4:
time: 77.3 us; the launch traced here: 77.1 us
  Pallas kernels  77.1 us (100%)
    pallas_call x1, Pallas kernels, per_device(): pl.pallas_call(exchange_kernel, out_shape=(jax.ShapeDtypeStruct((COUNTS[E...  71.3 us
    pallas_call x1, Pallas kernels, per_device(): pl.pallas_call(late_kernel, out_shape=jax.ShapeDtypeStruct((SLOTS, BLK, B...  5.79 us

profile of v4, /device:TPU:1, one launch (start us, length us, event | category | flops | bytes accessed | tf_op | source)
XLA Modules:
  0.0 77.1 jit_solution(587001709741738902)
XLA Ops:
  0.0 71.3 %shard_map.100 = (bf16[1,128,16,128]{3,2,1,0:T(8,128)(2,1)}, bf16[64,8,8,384]{3,2,1,0:T(8,128)(2,1)}, s32[16,128]{1,0:T(8,128)}) custom-call(bf16[960,4096]{1,0:T(8,128)(2,1)} %bitcast.3, bf16[1,64]{1,0:T(2,128)(2,1)} %bitcast.5, s32[2,4160]{1,0:T(2,128)} %bitcast.4, s32[4160]{0:T(1024)} %owner_hbm.1, bf16[192,208]{1,0:T(8,128)(2,1)} %constant.12.clone.basis_hbm, ...), custom_call_target="tpu_custom_call" | custom-call | tf_op jit(solution)/shard_map/pallas_call | solution.py:542
  71.3 5.8 %shard_map.101 = f32[64,8,8,384]{3,2,1,0:T(8,128)} custom-call(s32[16,128]{1,0:T(8,128)} %get-tuple-element.8.plan_ref, bf16[1,128,16,128]{3,2,1,0:T(8,128)(2,1)} %get-tuple-element.9.late_ref, bf16[64,8,8,384]{3,2,1,0:T(8,128)(2,1)} %get-tuple-element.10.partial_ref, bf16[256,384]{1,0:T(8,128)(2,1)} %constant.17.clone.lag_ref), custom_call_target="tpu_custom_call" | custom-call | tf_op jit(solution)/shard_map/pallas_call | solution.py:595

commit v5 on v4

--- a/solution.py
+++ b/solution.py
@@ -129,22 +129,21 @@
     return device // 8 % 4, device // 2 % 4, device // 32, device % 2
 
 
+def axis_of(turn, core):
+    return (turn + 2 * core) % 3
+
+
 def line_and_place(device, axis):
     z, x, y, c = coordinates(device)
-    if axis == 0:
-        return y * 8 + x * 2 + c, z
-    if axis == 1:
-        return y * 8 + z * 2 + c, x
-    return z * 8 + x * 2 + c, y
+    first, second = jnp.where(axis == 2, z, y), jnp.where(axis == 1, z, x)
+    return first * 8 + second * 2 + c, jnp.where(axis == 0, z, jnp.where(axis == 1, x, y))
 
 
 def device_of(line, place, axis):
     first, second, c = line // 8, line // 2 % 4, line % 2
-    if axis == 0:
-        return first * 32 + place * 8 + second * 2 + c
-    if axis == 1:
-        return first * 32 + second * 8 + place * 2 + c
-    return place * 32 + line
+    z = jnp.where(axis == 0, place, jnp.where(axis == 1, second, first))
+    x, y = jnp.where(axis == 1, place, second), jnp.where(axis == 2, place, first)
+    return y * 32 + z * 8 + x * 2 + c
 
 
 def make_plan(me, src, dst, own, plan_ref):
@@ -172,8 +171,8 @@
         second = second + jnp.where(hit, dst_dev[index : index + 1, :], 0)
     ends = jnp.sum(jnp.concatenate([first, second], axis=0).T, axis=0, keepdims=True)
     lines = []
-    for axis in range(3):
-        line, place = line_and_place(ends, axis)
+    for turn in range(3):
+        line, place = line_and_place(ends, axis_of(turn, ends % 2))
         lines.append(line * 4 + place)
     count = jnp.sum(flags, axis=(0, 1), keepdims=True)
     lines.append(jnp.broadcast_to(count, (1, 128)))
@@ -197,11 +196,11 @@
     lax.fori_loop(0, 12, wanted, 0)
 
 
-def cross_spectra(into, plan, cross, slot, tile, axes):
-    width = len(axes) * PIECE
-    for index, axis in enumerate(axes):
-        a = into[index, plan[12 + axis, slot]].astype(F32)
-        b = into[index, plan[12 + axis, SLOTS + slot]].astype(F32)
+def cross_spectra(into, plan, cross, slot, tile, turns):
+    width = len(turns) * PIECE
+    for index, turn in enumerate(turns):
+        a = into[index, plan[12 + turn, slot]].astype(F32)
+        b = into[index, plan[12 + turn, SLOTS + slot]].astype(F32)
         ar, ai, br, bi = a[:BLK], a[BLK:], b[:BLK], b[BLK:]
         left = index * PIECE
         for pair in range(BLK // 2):
@@ -217,7 +216,7 @@
             ).astype(BF16)
 
 
-def axes_of(part):
+def turns_of(part):
     return [piece % 3 for piece in range(CUTS[part], CUTS[part + 1])]
 
 
@@ -364,7 +363,8 @@
     gathered = gathered + (gathered4, gathered5, gathered6, gathered7)
     pl.semaphore_wait(plane_sem, GROUPS - 1)
     for piece in range(PIECES):
-        line, place = line_and_place(me, piece % 3)
+        axis = axis_of(piece % 3, core)
+        line, place = line_and_place(me, axis)
         bins = slice(piece * PIECE, (piece + 1) * PIECE)
         factor = scale[:, bins]
         parts = (acc[:, bins] * factor, acc[:, NF + piece * PIECE : NF + (piece + 1) * PIECE] * factor)
@@ -372,7 +372,7 @@
             [half.reshape(16, BLK, PIECE) for half in parts], axis=1
         ).astype(BF16)
         for step in (1, 3, 2):
-            to = device_of(line, (place + step) % 4, piece % 3)
+            to = device_of(line, (place + step) % 4, axis)
             pltpu.make_async_remote_copy(
                 src_ref=gathered[piece].at[place], dst_ref=gathered[piece].at[place],
                 send_sem=line_sem.at[piece], recv_sem=gather_sem.at[piece],
@@ -380,12 +380,12 @@
             ).start()
 
     def select(piece, to, out):
-        axis = piece % 3
+        axis = axis_of(piece % 3, core)
         for place in range(4):
             out[place] = gathered[piece][place, plan[4 * axis + place, to]]
 
     def emit(piece, part):
-        axis, index = piece % 3, piece - CUTS[part]
+        axis, index = axis_of(piece % 3, core), piece - CUTS[part]
         line, place = line_and_place(me, axis)
         first, second = line // 8, line // 2 % 4
 
@@ -439,7 +439,7 @@
     def tiles_of(part):
         def one(group, _):
             for tile in range(TILES):
-                cross_spectra(ins[part], plan, crosses[part], group * TILES + tile, tile, axes_of(part))
+                cross_spectra(ins[part], plan, crosses[part], group * TILES + tile, tile, turns_of(part))
             lagged = jnp.dot(crosses[part][...], lags[part][...], preferred_element_type=F32)
             lagged = lagged.reshape(TILES, BLK, BLK, NLAG)
             rows = pl.ds(group * TILES, TILES)
@@ -513,7 +513,7 @@
         @pl.when(group * TILES < count)
         def _():
             for tile in range(TILES):
-                cross_spectra(late, plan_ref, cross, group * TILES + tile, tile, axes_of(EARLY))
+                cross_spectra(late, plan_ref, cross, group * TILES + tile, tile, turns_of(EARLY))
             lagged = jnp.dot(cross[...], lag[...], preferred_element_type=F32)
             lagged = lagged + partial[rows(group)].astype(F32).reshape(lagged.shape)
             index = lax.broadcasted_iota(jnp.int32, lagged.shape, 0) // 64 + group * TILES

time: 77.3 us -> 78.2 us (1.012)
  Pallas kernels: 77.1 us -> 78.1 us
    pallas_call x1, Pallas kernels: 5.79 us -> 6.64 us  [per_device(): pl.pallas_call(late_kernel, out_shape=jax.ShapeDtypeStruct((SLOTS, BLK, B...]
where the time goes in v5:
time: 78.2 us; the launch traced here: 78.1 us
  Pallas kernels  78.1 us (100%)
    pallas_call x1, Pallas kernels, per_device(): pl.pallas_call(exchange_kernel, out_shape=(jax.ShapeDtypeStruct((COUNTS[E...  71.4 us
    pallas_call x1, Pallas kernels, per_device(): pl.pallas_call(late_kernel, out_shape=jax.ShapeDtypeStruct((SLOTS, BLK, B...  6.64 us

profile of v5, /device:TPU:1, one launch (start us, length us, event | category | flops | bytes accessed | tf_op | source)
XLA Modules:
  0.0 78.1 jit_solution(14119712001341485473)
XLA Ops:
  0.0 71.4 %shard_map.100 = (bf16[1,128,16,128]{3,2,1,0:T(8,128)(2,1)}, bf16[64,8,8,384]{3,2,1,0:T(8,128)(2,1)}, s32[16,128]{1,0:T(8,128)}) custom-call(bf16[960,4096]{1,0:T(8,128)(2,1)} %bitcast.3, bf16[1,64]{1,0:T(2,128)(2,1)} %bitcast.5, s32[2,4160]{1,0:T(2,128)} %bitcast.4, s32[4160]{0:T(1024)} %owner_hbm.1, bf16[192,208]{1,0:T(8,128)(2,1)} %constant.12.clone.basis_hbm, ...), custom_call_target="tpu_custom_call" | custom-call | tf_op jit(solution)/shard_map/pallas_call | solution.py:542
  71.4 6.6 %shard_map.101 = f32[64,8,8,384]{3,2,1,0:T(8,128)} custom-call(s32[16,128]{1,0:T(8,128)} %get-tuple-element.8.plan_ref, bf16[1,128,16,128]{3,2,1,0:T(8,128)(2,1)} %get-tuple-element.9.late_ref, bf16[64,8,8,384]{3,2,1,0:T(8,128)(2,1)} %get-tuple-element.10.partial_ref, bf16[256,384]{1,0:T(8,128)(2,1)} %constant.17.clone.lag_ref), custom_call_target="tpu_custom_call" | custom-call | tf_op jit(solution)/shard_map/pallas_call | solution.py:595

commit v6 on v4

--- a/solution.py
+++ b/solution.py
@@ -384,24 +384,48 @@
         for place in range(4):
             out[place] = gathered[piece][place, plan[4 * axis + place, to]]
 
+    def shifted(start, offset):
+        return lax.rem(start + jnp.where(core == 0, offset, 4 - offset), 4)
+
+    z_at, x_at = ([shifted(start, offset) for offset in range(4)] for start in (zc, xc))
+    mate = 1 - core
+
     def emit(piece, part):
         axis, index = piece % 3, piece - CUTS[part]
-        line, place = line_and_place(me, axis)
-        first, second = line // 8, line // 2 % 4
-
-        def one(step, _):
-            offset = step * 11 % 32
-            to_line = (first + turned(offset // 8)) % 4 * 8 + (second + turned(offset // 2 % 4)) % 4 * 2
-            to = device_of(to_line + (core + offset) % 2, place, axis)
-            select(piece, to, outs[part].at[index, step])
-            pltpu.make_async_remote_copy(
-                src_ref=outs[part].at[index, step], dst_ref=ins[part].at[index, pl.ds(line * 4, 4)],
-                send_sem=out_sem.at[part], recv_sem=in_sem.at[part],
-                device_id=(to // MEMBERS, to % MEMBERS), device_id_type=MESH,
-            ).start()
+        line, _ = line_and_place(me, axis)
+        second_at = z_at if axis == 1 else x_at
+
+        def eight(turn, _):
+            step = lax.rem(turn + 1, 4)
+            first = shifted(zc if axis == 2 else grp, step)
+            for offset in (1, 3, 2, 0):
+                second = second_at[offset]
+                for cross in range(2):
+                    to_core = mate if cross else core
+                    if axis == 0:
+                        to_grp, to_dev = first, zc * 8 + second * 2 + to_core
+                    elif axis == 1:
+                        to_grp, to_dev = first, second * 8 + xc * 2 + to_core
+                    else:
+                        to_grp, to_dev = grp, first * 8 + second * 2 + to_core
+                    slot = step * 8 + (offset * 2 + cross)
+
+                    def send_one(to_grp=to_grp, to_dev=to_dev, slot=slot):
+                        out = outs[part].at[index, slot]
+                        select(piece, to_grp * MEMBERS + to_dev, out)
+                        pltpu.make_async_remote_copy(
+                            src_ref=out, dst_ref=ins[part].at[index, pl.ds(line * 4, 4)],
+                            send_sem=out_sem.at[part], recv_sem=in_sem.at[part],
+                            device_id=(to_grp, to_dev), device_id_type=MESH,
+                        ).start()
+
+                    if offset == 0 and cross == 0:
+                        pl.when(step != 0)(send_one)
+                    else:
+                        send_one()
             return 0
 
-        lax.fori_loop(1, MEMBERS, one, 0)
+        lax.fori_loop(0, 4, eight, 0)
         select(piece, me, outs[part].at[index, 0])
         return pltpu.make_async_copy(
             outs[part].at[index, 0], ins[part].at[index, pl.ds(line * 4, 4)], own_sem.at[piece]

time: 77.3 us -> 75.9 us (0.982)
  Pallas kernels: 77.1 us -> 75.6 us
    pallas_call x1, Pallas kernels: 71.3 us -> 69.8 us  [per_device(): pl.pallas_call(exchange_kernel, out_shape=(jax.ShapeDtypeStruct((COUNTS[E...]
where the time goes in v6:
time: 75.9 us; the launch traced here: 75.6 us
  Pallas kernels  75.6 us (100%)
    pallas_call x1, Pallas kernels, per_device(): pl.pallas_call(exchange_kernel, out_shape=(jax.ShapeDtypeStruct((COUNTS[E...  69.8 us
    pallas_call x1, Pallas kernels, per_device(): pl.pallas_call(late_kernel, out_shape=jax.ShapeDtypeStruct((SLOTS, BLK, B...  5.79 us

profile of v6, /device:TPU:1, one launch (start us, length us, event | category | flops | bytes accessed | tf_op | source)
XLA Modules:
  0.0 75.6 jit_solution(9138047986755780260)
XLA Ops:
  0.0 69.8 %shard_map.100 = (bf16[1,128,16,128]{3,2,1,0:T(8,128)(2,1)}, bf16[64,8,8,384]{3,2,1,0:T(8,128)(2,1)}, s32[16,128]{1,0:T(8,128)}) custom-call(bf16[960,4096]{1,0:T(8,128)(2,1)} %bitcast.3, bf16[1,64]{1,0:T(2,128)(2,1)} %bitcast.5, s32[2,4160]{1,0:T(2,128)} %bitcast.4, s32[4160]{0:T(1024)} %owner_hbm.1, bf16[192,208]{1,0:T(8,128)(2,1)} %constant.12.clone.basis_hbm, ...), custom_call_target="tpu_custom_call" | custom-call | tf_op jit(solution)/shard_map/pallas_call | solution.py:566
  69.8 5.8 %shard_map.101 = f32[64,8,8,384]{3,2,1,0:T(8,128)} custom-call(s32[16,128]{1,0:T(8,128)} %get-tuple-element.8.plan_ref, bf16[1,128,16,128]{3,2,1,0:T(8,128)(2,1)} %get-tuple-element.9.late_ref, bf16[64,8,8,384]{3,2,1,0:T(8,128)(2,1)} %get-tuple-element.10.partial_ref, bf16[256,384]{1,0:T(8,128)(2,1)} %constant.17.clone.lag_ref), custom_call_target="tpu_custom_call" | custom-call | tf_op jit(solution)/shard_map/pallas_call | solution.py:619

commit v7 on v6

--- a/solution.py
+++ b/solution.py
@@ -30,6 +30,7 @@
 SLOTS = 64
 PIECE = 128
 PIECES = NF // PIECE
+AHEAD = 3
 CUTS = (0, 4, 6, 7, 8)
 COUNTS = (4, 2, 1, 1)
 EARLY = len(COUNTS) - 1
@@ -362,6 +363,28 @@
     crosses, lags = (cross0, cross1, cross2), (lag0, lag1, lag2)
     gathered = (gathered0, gathered1, gathered2, gathered3)
     gathered = gathered + (gathered4, gathered5, gathered6, gathered7)
+    def line_copy(piece, source, blocks, way, sem):
+        line, place = line_and_place(me, piece % 3)
+        to = device_of(line, lax.rem(place + (1, 3)[way], 4), piece % 3)
+        view = gathered[piece].at[source, blocks]
+        return pltpu.make_async_remote_copy(
+            src_ref=view, dst_ref=view, send_sem=line_sem.at[piece], recv_sem=gather_sem.at[piece, sem],
+            device_id=(to // MEMBERS, to % MEMBERS), device_id_type=MESH,
+        )
+
+    def near(piece, way):
+        _, place = line_and_place(me, piece % 3)
+        return line_copy(piece, place, pl.ds(0, 16), way, way)
+
+    def onward(piece, way):
+        _, place = line_and_place(me, piece % 3)
+        return line_copy(piece, lax.rem(place + (3, 1)[way], 4), pl.ds(8 * way, 8), way, 2 + way)
+
+    def pass_on(piece):
+        for way in range(2):
+            near(piece, way).wait_recv()
+            onward(piece, way).start()
+
     pl.semaphore_wait(plane_sem, GROUPS - 1)
     for piece in range(PIECES):
         line, place = line_and_place(me, piece % 3)
@@ -371,13 +394,8 @@
         gathered[piece][place] = jnp.concatenate(
             [half.reshape(16, BLK, PIECE) for half in parts], axis=1
         ).astype(BF16)
-        for step in (1, 3, 2):
-            to = device_of(line, (place + step) % 4, piece % 3)
-            pltpu.make_async_remote_copy(
-                src_ref=gathered[piece].at[place], dst_ref=gathered[piece].at[place],
-                send_sem=line_sem.at[piece], recv_sem=gather_sem.at[piece],
-                device_id=(to // MEMBERS, to % MEMBERS), device_id_type=MESH,
-            ).start()
+        for way in range(2):
+            near(piece, way).start()
 
     def select(piece, to, out):
         axis = piece % 3
@@ -441,11 +459,15 @@
     plan_out = pltpu.make_async_copy(plan_vector, plan_out_ref, plan_out_sem)
     plan_out.start()
     plan_copy.wait()
+    for piece in range(AHEAD):
+        pass_on(piece)
     own_copies = []
     for part in range(EARLY + 1):
         for piece in range(CUTS[part], CUTS[part + 1]):
-            others = gathered[piece].at[pl.ds(0, 3)]
-            pltpu.make_async_copy(others, others, gather_sem.at[piece]).wait()
+            if piece + AHEAD < PIECES:
+                pass_on(piece + AHEAD)
+            for way in range(2):
+                onward(piece, way).wait_recv()
             own_copies.append(emit(piece, part))
             own_copies[piece].start()
 
@@ -601,7 +623,7 @@
             pltpu.SemaphoreType.DMA((MEMBERS,)),
             pltpu.SemaphoreType.DMA((MEMBERS,)),
             pltpu.SemaphoreType.DMA((PIECES,)),
-            pltpu.SemaphoreType.DMA((PIECES,)),
+            pltpu.SemaphoreType.DMA((PIECES, 4)),
             pltpu.SemaphoreType.DMA((EARLY + 1,)),
             pltpu.SemaphoreType.DMA((EARLY + 1,)),
             pltpu.SemaphoreType.DMA((PIECES,)),

time: 75.9 us -> 80.9 us (1.066)
  Pallas kernels: 75.6 us -> 80.2 us
    pallas_call x1, Pallas kernels: 69.8 us -> 74.2 us  [per_device(): pl.pallas_call(exchange_kernel, out_shape=(jax.ShapeDtypeStruct((COUNTS[E...]
where the time goes in v7:
time: 80.9 us; the launch traced here: 80.2 us
  Pallas kernels  80.2 us (99%)
    pallas_call x1, Pallas kernels, per_device(): pl.pallas_call(exchange_kernel, out_shape=(jax.ShapeDtypeStruct((COUNTS[E...  74.2 us
    pallas_call x1, Pallas kernels, per_device(): pl.pallas_call(late_kernel, out_shape=jax.ShapeDtypeStruct((SLOTS, BLK, B...  5.99 us

profile of v7, /device:TPU:1, one launch (start us, length us, event | category | flops | bytes accessed | tf_op | source)
XLA Modules:
  0.0 80.2 jit_solution(762100228529546117)
XLA Ops:
  0.0 74.2 %shard_map.100 = (bf16[1,128,16,128]{3,2,1,0:T(8,128)(2,1)}, bf16[64,8,8,384]{3,2,1,0:T(8,128)(2,1)}, s32[16,128]{1,0:T(8,128)}) custom-call(bf16[960,4096]{1,0:T(8,128)(2,1)} %bitcast.3, bf16[1,64]{1,0:T(2,128)(2,1)} %bitcast.5, s32[2,4160]{1,0:T(2,128)} %bitcast.4, s32[4160]{0:T(1024)} %owner_hbm.1, bf16[192,208]{1,0:T(8,128)(2,1)} %constant.12.clone.basis_hbm, ...), custom_call_target="tpu_custom_call" | custom-call | tf_op jit(solution)/shard_map/pallas_call | solution.py:588
  74.2 6.0 %shard_map.101 = f32[64,8,8,384]{3,2,1,0:T(8,128)} custom-call(s32[16,128]{1,0:T(8,128)} %get-tuple-element.8.plan_ref, bf16[1,128,16,128]{3,2,1,0:T(8,128)(2,1)} %get-tuple-element.9.late_ref, bf16[64,8,8,384]{3,2,1,0:T(8,128)(2,1)} %get-tuple-element.10.partial_ref, bf16[256,384]{1,0:T(8,128)(2,1)} %constant.17.clone.lag_ref), custom_call_target="tpu_custom_call" | custom-call | tf_op jit(solution)/shard_map/pallas_call | solution.py:641

commit v8 on v6

--- a/solution.py
+++ b/solution.py
@@ -177,31 +177,34 @@
         lines.append(line * 4 + place)
     count = jnp.sum(flags, axis=(0, 1), keepdims=True)
     lines.append(jnp.broadcast_to(count, (1, 128)))
-    plan_ref[12:16, :] = jnp.concatenate(lines, axis=0)
+    lines.append(jnp.zeros((1, 128), jnp.int32))
+    plan_ref[3:8, :] = jnp.concatenate(lines, axis=0)
 
     z, x, y, _ = coordinates(me)
-
-    def wanted(entry, _):
-        axis, place = entry // 4, entry % 4
-        source = jnp.where(
-            axis == 0, me + (place - z) * 8, jnp.where(axis == 1, me + (place - x) * 2, me + (place - y) * 32)
-        )
-        local = jnp.where(src_dev == source, src % 16, 0) + jnp.where(dst_dev == source, dst % 16, 0)
-        blocks = jnp.zeros((128, 128), jnp.int32)
-        for index in range(rows):
-            hit = own[index : index + 1, :] == lane_a
-            blocks = blocks + jnp.where(hit, local[index : index + 1, :], 0)
-        plan_ref[pl.ds(entry, 1), :] = jnp.sum(blocks.T, axis=0, keepdims=True)
-        return 0
-
-    lax.fori_loop(0, 12, wanted, 0)
+    tables = []
+    for axis in range(3):
+        line, place = line_and_place(own, axis)
+        _, my_place = line_and_place(me, axis)
+        line = jnp.where(place == my_place, line, -1)
+        start, stride = ((z, 8), (x, 2), (y, 32))[axis]
+        blocks = []
+        for other in range(4):
+            source = me + (other - start) * stride
+            local = jnp.where(src_dev == source, src % 16, 0) + jnp.where(dst_dev == source, dst % 16, 0)
+            total = jnp.zeros((32, 128), jnp.int32)
+            for index in range(rows):
+                hit = line[index : index + 1, :] == lane_a[:32]
+                total = total + jnp.where(hit, local[index : index + 1, :], 0)
+            blocks.append(total)
+        tables.append(jnp.sum(jnp.concatenate(blocks, axis=0).T, axis=0, keepdims=True))
+    plan_ref[0:3, :] = jnp.concatenate(tables, axis=0)
 
 
 def cross_spectra(into, plan, cross, slot, tile, axes):
     width = len(axes) * PIECE
     for index, axis in enumerate(axes):
-        a = into[index, plan[12 + axis, slot]].astype(F32)
-        b = into[index, plan[12 + axis, SLOTS + slot]].astype(F32)
+        a = into[index, plan[3 + axis, slot]].astype(F32)
+        b = into[index, plan[3 + axis, SLOTS + slot]].astype(F32)
         ar, ai, br, bi = a[:BLK], a[BLK:], b[:BLK], b[BLK:]
         left = index * PIECE
         for pair in range(BLK // 2):
@@ -379,10 +382,10 @@
                 device_id=(to // MEMBERS, to % MEMBERS), device_id_type=MESH,
             ).start()
 
-    def select(piece, to, out):
+    def select(piece, to_line, out):
         axis = piece % 3
         for place in range(4):
-            out[place] = gathered[piece][place, plan[4 * axis + place, to]]
+            out[place] = gathered[piece][place, plan[axis, 32 * place + to_line]]
 
     def shifted(start, offset):
         return lax.rem(start + jnp.where(core == 0, offset, 4 - offset), 4)
@@ -408,11 +411,12 @@
                         to_grp, to_dev = first, second * 8 + xc * 2 + to_core
                     else:
                         to_grp, to_dev = grp, first * 8 + second * 2 + to_core
+                    to_line = first * 8 + second * 2 + to_core
                     slot = step * 8 + (offset * 2 + cross)
 
-                    def send_one(to_grp=to_grp, to_dev=to_dev, slot=slot):
+                    def send_one(to_grp=to_grp, to_dev=to_dev, to_line=to_line, slot=slot):
                         out = outs[part].at[index, slot]
-                        select(piece, to_grp * MEMBERS + to_dev, out)
+                        select(piece, to_line, out)
                         pltpu.make_async_remote_copy(
                             src_ref=out, dst_ref=ins[part].at[index, pl.ds(line * 4, 4)],
                             send_sem=out_sem.at[part], recv_sem=in_sem.at[part],
@@ -426,7 +430,7 @@
             return 0
 
         lax.fori_loop(0, 4, eight, 0)
-        select(piece, me, outs[part].at[index, 0])
+        select(piece, line, outs[part].at[index, 0])
         return pltpu.make_async_copy(
             outs[part].at[index, 0], ins[part].at[index, pl.ds(line * 4, 4)], own_sem.at[piece]
         )
@@ -498,7 +502,7 @@
     plan_ref, late_ref, partial_ref, lag_ref, out_ref,
     late, lag, partial, total, cross, late_sem, lag_sem, in_sem, out_sem,
 ):
-    count = plan_ref[15, 0]
+    count = plan_ref[6, 0]
     pieces = 4
     size = DEVICES // pieces
     late_copies = [
@@ -568,7 +572,7 @@
         out_shape=(
             jax.ShapeDtypeStruct((COUNTS[EARLY], DEVICES, 2 * BLK, PIECE), BF16),
             jax.ShapeDtypeStruct((SLOTS, BLK, BLK, NLAG), BF16),
-            jax.ShapeDtypeStruct((16, 128), jnp.int32),
+            jax.ShapeDtypeStruct((8, 128), jnp.int32),
         ),
         in_specs=[hbm] * (6 + EARLY),
         out_specs=(hbm, hbm, hbm),
@@ -581,8 +585,8 @@
             pltpu.VMEM((4, 8 * RANK, 2 * NF), BF16),
             *[pltpu.VMEM((2 * count * PIECE, NLAG), BF16) for count in COUNTS[:EARLY]],
             pltpu.VMEM((EXT, 960), BF16),
-            pltpu.VMEM((16, 128), jnp.int32),
-            pltpu.SMEM((16, 128), jnp.int32),
+            pltpu.VMEM((8, 128), jnp.int32),
+            pltpu.SMEM((8, 128), jnp.int32),
             pltpu.VMEM((MEMBERS, RANK, CH), BF16),
             pltpu.VMEM((MEMBERS, RANK, CH), BF16),
             pltpu.VMEM((CH, 2 * NF), F32),

time: 75.9 us -> 77.3 us (1.018)
    pallas_call x1, Pallas kernels: 69.8 us -> 70.8 us  [per_device(): pl.pallas_call(exchange_kernel, out_shape=(jax.ShapeDtypeStruct((COUNTS[E...]
where the time goes in v8:
time: 77.3 us; the launch traced here: 76.3 us
  Pallas kernels  76.3 us (99%)
    pallas_call x1, Pallas kernels, per_device(): pl.pallas_call(exchange_kernel, out_shape=(jax.ShapeDtypeStruct((COUNTS[E...  70.8 us
    pallas_call x1, Pallas kernels, per_device(): pl.pallas_call(late_kernel, out_shape=jax.ShapeDtypeStruct((SLOTS, BLK, B...  5.52 us

profile of v8, /device:TPU:1, one launch (start us, length us, event | category | flops | bytes accessed | tf_op | source)
XLA Modules:
  0.0 76.3 jit_solution(15205507750924791463)
XLA Ops:
  0.0 70.8 %shard_map.100 = (bf16[1,128,16,128]{3,2,1,0:T(8,128)(2,1)}, bf16[64,8,8,384]{3,2,1,0:T(8,128)(2,1)}, s32[8,128]{1,0:T(8,128)}) custom-call(bf16[960,4096]{1,0:T(8,128)(2,1)} %bitcast.3, bf16[1,64]{1,0:T(2,128)(2,1)} %bitcast.5, s32[2,4160]{1,0:T(2,128)} %bitcast.4, s32[4160]{0:T(1024)} %owner_hbm.1, bf16[192,208]{1,0:T(8,128)(2,1)} %constant.12.clone.basis_hbm, ...), custom_call_target="tpu_custom_call" | custom-call | tf_op jit(solution)/shard_map/pallas_call | solution.py:570
  70.8 5.5 %shard_map.101 = f32[64,8,8,384]{3,2,1,0:T(8,128)} custom-call(s32[8,128]{1,0:T(8,128)} %get-tuple-element.8.plan_ref, bf16[1,128,16,128]{3,2,1,0:T(8,128)(2,1)} %get-tuple-element.9.late_ref, bf16[64,8,8,384]{3,2,1,0:T(8,128)(2,1)} %get-tuple-element.10.partial_ref, bf16[256,384]{1,0:T(8,128)(2,1)} %constant.17.clone.lag_ref), custom_call_target="tpu_custom_call" | custom-call | tf_op jit(solution)/shard_map/pallas_call | solution.py:623

commit v9 on v6

--- a/solution.py
+++ b/solution.py
@@ -34,6 +34,7 @@
 COUNTS = (4, 2, 1, 1)
 EARLY = len(COUNTS) - 1
 TILES = 4
+LATE_TILES = 8
 MESH = pl.DeviceIdType.MESH
 F32 = jnp.float32
 BF16 = jnp.bfloat16
@@ -511,7 +512,7 @@
     lag_copy = pltpu.make_async_copy(lag_ref, lag, lag_sem)
 
     def rows(group):
-        return pl.ds(group * TILES, TILES)
+        return pl.ds(group * LATE_TILES, LATE_TILES)
 
     def load(group):
         return pltpu.make_async_copy(
@@ -526,7 +527,7 @@
         load(group).start()
         return 0
 
-    lax.fori_loop(0, SLOTS // TILES, fetch, 0)
+    lax.fori_loop(0, SLOTS // LATE_TILES, fetch, 0)
     for copy in late_copies:
         copy.wait()
     lag_copy.wait()
@@ -534,23 +535,23 @@
     def one(group, _):
         load(group).wait()
 
-        @pl.when(group * TILES < count)
+        @pl.when(group * LATE_TILES < count)
         def _():
-            for tile in range(TILES):
-                cross_spectra(late, plan_ref, cross, group * TILES + tile, tile, axes_of(EARLY))
+            for tile in range(LATE_TILES):
+                cross_spectra(late, plan_ref, cross, group * LATE_TILES + tile, tile, axes_of(EARLY))
             lagged = jnp.dot(cross[...], lag[...], preferred_element_type=F32)
             lagged = lagged + partial[rows(group)].astype(F32).reshape(lagged.shape)
-            index = lax.broadcasted_iota(jnp.int32, lagged.shape, 0) // 64 + group * TILES
-            total[rows(group)] = jnp.where(index < count, lagged, 0.0).reshape(TILES, BLK, BLK, NLAG)
-
-        @pl.when(group * TILES >= count)
+            index = lax.broadcasted_iota(jnp.int32, lagged.shape, 0) // 64 + group * LATE_TILES
+            total[rows(group)] = jnp.where(index < count, lagged, 0.0).reshape(LATE_TILES, BLK, BLK, NLAG)
+
+        @pl.when(group * LATE_TILES >= count)
         def _():
-            total[rows(group)] = jnp.zeros((TILES, BLK, BLK, NLAG), F32)
+            total[rows(group)] = jnp.zeros((LATE_TILES, BLK, BLK, NLAG), F32)
 
         pltpu.make_async_copy(total.at[rows(group)], out_ref.at[rows(group)], out_sem).start()
         return 0
 
-    lax.fori_loop(0, SLOTS // TILES, one, 0)
+    lax.fori_loop(0, SLOTS // LATE_TILES, one, 0)
     pltpu.make_async_copy(total, out_ref, out_sem).wait()
 
 
@@ -562,7 +563,6 @@
         lag.reshape(2, PIECES, PIECE, NLAG)[:, CUTS[part] : CUTS[part + 1]].reshape(-1, NLAG)
         for part in range(EARLY + 1)
     ]
-    groups = SLOTS // TILES
     late, partial, plan = pl.pallas_call(
         exchange_kernel,
         out_shape=(
@@ -626,10 +626,10 @@
             pltpu.VMEM((2 * COUNTS[EARLY] * PIECE, NLAG), BF16),
             pltpu.VMEM((SLOTS, BLK, BLK, NLAG), BF16),
             pltpu.VMEM((SLOTS, BLK, BLK, NLAG), F32),
-            pltpu.VMEM((TILES * 64, 2 * COUNTS[EARLY] * PIECE), BF16),
+            pltpu.VMEM((LATE_TILES * 64, 2 * COUNTS[EARLY] * PIECE), BF16),
             pltpu.SemaphoreType.DMA((4,)),
             pltpu.SemaphoreType.DMA,
-            pltpu.SemaphoreType.DMA((groups,)),
+            pltpu.SemaphoreType.DMA((SLOTS // LATE_TILES,)),
             pltpu.SemaphoreType.DMA,
         ],
         compiler_params=pltpu.CompilerParams(vmem_limit_bytes=60 * 2**20),

time: 75.9 us -> 75.3 us (level)
  no operation moved by 1% of the time
where the time goes in v9:
time: 75.3 us; the launch traced here: 75.1 us
  Pallas kernels  75.1 us (100%)
    pallas_call x1, Pallas kernels, per_device(): pl.pallas_call(exchange_kernel, out_shape=(jax.ShapeDtypeStruct((COUNTS[E...  69.8 us
    pallas_call x1, Pallas kernels, per_device(): pl.pallas_call(late_kernel, out_shape=jax.ShapeDtypeStruct((SLOTS, BLK, B...  5.22 us

profile of v9, /device:TPU:1, one launch (start us, length us, event | category | flops | bytes accessed | tf_op | source)
XLA Modules:
  0.0 75.1 jit_solution(12865913069541789691)
XLA Ops:
  0.0 69.8 %shard_map.100 = (bf16[1,128,16,128]{3,2,1,0:T(8,128)(2,1)}, bf16[64,8,8,384]{3,2,1,0:T(8,128)(2,1)}, s32[16,128]{1,0:T(8,128)}) custom-call(bf16[960,4096]{1,0:T(8,128)(2,1)} %bitcast.3, bf16[1,64]{1,0:T(2,128)(2,1)} %bitcast.5, s32[2,4160]{1,0:T(2,128)} %bitcast.4, s32[4160]{0:T(1024)} %owner_hbm.1, bf16[192,208]{1,0:T(8,128)(2,1)} %constant.12.clone.basis_hbm, ...), custom_call_target="tpu_custom_call" | custom-call | tf_op jit(solution)/shard_map/pallas_call | solution.py:566
  69.9 5.2 %shard_map.101 = f32[64,8,8,384]{3,2,1,0:T(8,128)} custom-call(s32[16,128]{1,0:T(8,128)} %get-tuple-element.8.plan_ref, bf16[1,128,16,128]{3,2,1,0:T(8,128)(2,1)} %get-tuple-element.9.late_ref, bf16[64,8,8,384]{3,2,1,0:T(8,128)(2,1)} %get-tuple-element.10.partial_ref, bf16[256,384]{1,0:T(8,128)(2,1)} %constant.17.clone.lag_ref), custom_call_target="tpu_custom_call" | custom-call | tf_op jit(solution)/shard_map/pallas_call | solution.py:619

commit v10 on v9

--- a/solution.py
+++ b/solution.py
@@ -130,22 +130,21 @@
     return device // 8 % 4, device // 2 % 4, device // 32, device % 2
 
 
+def axis_of(turn, core):
+    return (turn + 2 * core) % 3
+
+
 def line_and_place(device, axis):
     z, x, y, c = coordinates(device)
-    if axis == 0:
-        return y * 8 + x * 2 + c, z
-    if axis == 1:
-        return y * 8 + z * 2 + c, x
-    return z * 8 + x * 2 + c, y
+    first, second = jnp.where(axis == 2, z, y), jnp.where(axis == 1, z, x)
+    return first * 8 + second * 2 + c, jnp.where(axis == 0, z, jnp.where(axis == 1, x, y))
 
 
 def device_of(line, place, axis):
     first, second, c = line // 8, line // 2 % 4, line % 2
-    if axis == 0:
-        return first * 32 + place * 8 + second * 2 + c
-    if axis == 1:
-        return first * 32 + second * 8 + place * 2 + c
-    return place * 32 + line
+    z = jnp.where(axis == 0, place, jnp.where(axis == 1, second, first))
+    x, y = jnp.where(axis == 1, place, second), jnp.where(axis == 2, place, first)
+    return y * 32 + z * 8 + x * 2 + c
 
 
 def make_plan(me, src, dst, own, plan_ref):
@@ -173,8 +172,8 @@
         second = second + jnp.where(hit, dst_dev[index : index + 1, :], 0)
     ends = jnp.sum(jnp.concatenate([first, second], axis=0).T, axis=0, keepdims=True)
     lines = []
-    for axis in range(3):
-        line, place = line_and_place(ends, axis)
+    for turn in range(3):
+        line, place = line_and_place(ends, axis_of(turn, ends % 2))
         lines.append(line * 4 + place)
     count = jnp.sum(flags, axis=(0, 1), keepdims=True)
     lines.append(jnp.broadcast_to(count, (1, 128)))
@@ -365,7 +364,8 @@
     gathered = gathered + (gathered4, gathered5, gathered6, gathered7)
     pl.semaphore_wait(plane_sem, GROUPS - 1)
     for piece in range(PIECES):
-        line, place = line_and_place(me, piece % 3)
+        axis = axis_of(piece % 3, core)
+        line, place = line_and_place(me, axis)
         bins = slice(piece * PIECE, (piece + 1) * PIECE)
         factor = scale[:, bins]
         parts = (acc[:, bins] * factor, acc[:, NF + piece * PIECE : NF + (piece + 1) * PIECE] * factor)
@@ -373,7 +373,7 @@
             [half.reshape(16, BLK, PIECE) for half in parts], axis=1
         ).astype(BF16)
         for step in (1, 3, 2):
-            to = device_of(line, (place + step) % 4, piece % 3)
+            to = device_of(line, (place + step) % 4, axis)
             pltpu.make_async_remote_copy(
                 src_ref=gathered[piece].at[place], dst_ref=gathered[piece].at[place],
                 send_sem=line_sem.at[piece], recv_sem=gather_sem.at[piece],
@@ -381,7 +381,7 @@
             ).start()
 
     def select(piece, to, out):
-        axis = piece % 3
+        axis = axis_of(piece % 3, core)
         for place in range(4):
             out[place] = gathered[piece][place, plan[4 * axis + place, to]]
 
@@ -392,26 +392,23 @@
     mate = 1 - core
 
     def emit(piece, part):
-        axis, index = piece % 3, piece - CUTS[part]
+        axis, index = axis_of(piece % 3, core), piece - CUTS[part]
         line, _ = line_and_place(me, axis)
-        second_at = z_at if axis == 1 else x_at
+        second_at = [jnp.where(axis == 1, z, x) for z, x in zip(z_at, x_at)]
 
         def eight(turn, _):
             step = lax.rem(turn + 1, 4)
-            first = shifted(zc if axis == 2 else grp, step)
+            first = shifted(jnp.where(axis == 2, zc, grp), step)
+            to_grp = jnp.where(axis == 2, grp, first)
             for offset in (1, 3, 2, 0):
                 second = second_at[offset]
+                near = jnp.where(axis == 0, zc, jnp.where(axis == 1, second, first)) * 8
+                near = near + jnp.where(axis == 1, xc, second) * 2
                 for cross in range(2):
-                    to_core = mate if cross else core
-                    if axis == 0:
-                        to_grp, to_dev = first, zc * 8 + second * 2 + to_core
-                    elif axis == 1:
-                        to_grp, to_dev = first, second * 8 + xc * 2 + to_core
-                    else:
-                        to_grp, to_dev = grp, first * 8 + second * 2 + to_core
+                    to_dev = near + (mate if cross else core)
                     slot = step * 8 + (offset * 2 + cross)
 
-                    def send_one(to_grp=to_grp, to_dev=to_dev, slot=slot):
+                    def send_one(to_dev=to_dev, slot=slot):
                         out = outs[part].at[index, slot]
                         select(piece, to_grp * MEMBERS + to_dev, out)
                         pltpu.make_async_remote_copy(

time: 75.3 us -> 77.6 us (1.031)
  the two profiles are of different devices: /device:TPU:1 before, /device:TPU:48 now
where the time goes in v10:
time: 77.6 us; the launch traced here: 77.5 us
  Pallas kernels  77.4 us (100%)
    pallas_call x1, Pallas kernels, per_device(): pl.pallas_call(exchange_kernel, out_shape=(jax.ShapeDtypeStruct((COUNTS[E...  71.7 us
    pallas_call x1, Pallas kernels, per_device(): pl.pallas_call(late_kernel, out_shape=jax.ShapeDtypeStruct((SLOTS, BLK, B...  5.72 us

profile of v10, /device:TPU:48, one launch (start us, length us, event | category | flops | bytes accessed | tf_op | source)
XLA Modules:
  0.0 77.5 jit_solution(17143889419858209088)
XLA Ops:
  0.0 71.7 %shard_map.100 = (bf16[1,128,16,128]{3,2,1,0:T(8,128)(2,1)}, bf16[64,8,8,384]{3,2,1,0:T(8,128)(2,1)}, s32[16,128]{1,0:T(8,128)}) custom-call(bf16[960,4096]{1,0:T(8,128)(2,1)} %bitcast.3, bf16[1,64]{1,0:T(2,128)(2,1)} %bitcast.5, s32[2,4160]{1,0:T(2,128)} %bitcast.4, s32[4160]{0:T(1024)} %owner_hbm.1, bf16[192,208]{1,0:T(8,128)(2,1)} %constant.12.clone.basis_hbm, ...), custom_call_target="tpu_custom_call" | custom-call | tf_op jit(solution)/shard_map/pallas_call | solution.py:563
  71.7 5.7 %shard_map.101 = f32[64,8,8,384]{3,2,1,0:T(8,128)} custom-call(s32[16,128]{1,0:T(8,128)} %get-tuple-element.8.plan_ref, bf16[1,128,16,128]{3,2,1,0:T(8,128)(2,1)} %get-tuple-element.9.late_ref, bf16[64,8,8,384]{3,2,1,0:T(8,128)(2,1)} %get-tuple-element.10.partial_ref, bf16[256,384]{1,0:T(8,128)(2,1)} %constant.17.clone.lag_ref), custom_call_target="tpu_custom_call" | custom-call | tf_op jit(solution)/shard_map/pallas_call | solution.py:616
